TPU v7x, 128 devices: a whole 4x4x4 slice. The times are simulated.
128 devices in a mesh: sect: 8 (over z, core), dev: 16 (over x, y).
Axes of the slice: x: 4, y: 4, z: 4, core: 2. Of those that a mesh axis runs over, the one named last changes fastest.
Arguments:
- points: float32 [3, 2097152], P(None, ('sect', 'dev')), may hold values from 0 to 1
- vectors: bfloat16 [8, 2097152], P(None, ('sect', 'dev')), may hold values from -6 to 6
- near_list: int32 [8192, 16], P(('sect', 'dev')), may hold values from 0 to 8191, as said below
- near_count: int32 [8192], P(('sect', 'dev')), may hold values from 1 to 16, as said below
- couple_list: int32 [8192, 16], P(('sect', 'dev')), may hold values from 0 to 8191, as said below
- leaf_basis: bfloat16 [8192, 64, 256], P(('sect', 'dev')), may hold values from -0.375 to 0.375
- local_transfer: bfloat16 [128, 126, 4096], P(('sect', 'dev')), may hold values from -0.625 to 0.625
- couple_block: bfloat16 [8192, 16, 4096], P(('sect', 'dev')), may hold values from -0.1875 to 0.1875
- upper_transfer: bfloat16 [256, 4096], P(('sect', 'dev')), may hold values from -0.625 to 0.625
- upper_couple: bfloat16 [256, 3, 4096], P(('sect', 'dev')), may hold values from -0.4375 to 0.4375
Outputs:
- product: float32 [8, 2097152], P(None, ('sect', 'dev'))
Inputs may be any that keep to these rules, and one draw needn't show every extreme that they name: `near_list`: row l names 16 different leaves other than l, each held by the device that holds l or by one of the two devices next to it in the order of devices. The leading near_count[l] entries of row l of near_list are the near-field partners of leaf l. `couple_list`: row l names 16 different leaves other than l, each held by a device at most 2 places from the one that holds l in the order of devices.
All inputs are finite; a program needn't handle non-finite values.
Results may differ from a plain program's by a relative error of at most 0.03.
Values may be sent and summed in bfloat16 or wider, within the bound.
A program may use at most 128 MiB of HBM per device.

v0:
```python
import math

import jax
import jax.numpy as jnp
from jax import lax
from jax.sharding import PartitionSpec as P

REACH = 2


soft_sq = 0.0025
even_offsets = (-2, 2, 3)
odd_offsets = (-3, -2, 2)


def from_behind(block, axis, distance):
    devices = range(lax.axis_size(axis))
    route = [(i - distance, i) for i in devices if i - distance in devices]
    return lax.ppermute(block, axis, route)


def batched(left, right):
    return jnp.einsum("nvr,nrs->nvs", left, right, preferred_element_type=jnp.float32)


def batched_back(left, right):
    return jnp.einsum("nvs,nrs->nvr", left, right, preferred_element_type=jnp.float32)


def kernel_block(source, target, kernel_scale):
    delta_x = source[0][:, :, None] - target[0][:, None, :]
    delta_y = source[1][:, :, None] - target[1][:, None, :]
    delta_z = source[2][:, :, None] - target[2][:, None, :]
    distance_sq = delta_x * delta_x + delta_y * delta_y + delta_z * delta_z
    return (lax.rsqrt(distance_sq + soft_sq) * kernel_scale).astype(jnp.bfloat16)


def near_product(source_vectors, kernel):
    return jnp.einsum("vnq,nqp->vnp", source_vectors, kernel, preferred_element_type=jnp.float32)


def shards(
    points,
    vectors,
    near_list,
    near_count,
    couple_list,
    leaf_basis,
    local_transfer,
    couple_block,
    upper_transfer,
    upper_couple,
):
    devices = lax.axis_size(("sect", "dev"))
    my_index = lax.axis_index(("sect", "dev"))
    leaves = leaf_basis.shape[0]
    rank = leaf_basis.shape[1]
    leaf_size = leaf_basis.shape[2]
    vec_count = vectors.shape[0]
    near_slots = near_list.shape[1]
    couple_slots = couple_list.shape[1]
    levels = leaves.bit_length() - 1
    top_levels = devices.bit_length() - 1
    moved_points = {}
    moved_vectors = {}
    for side_shift in (1, -1):
        moved_points[side_shift] = from_behind(points, ("sect", "dev"), side_shift)
        moved_vectors[side_shift] = from_behind(vectors, ("sect", "dev"), side_shift)
    window_points = jnp.concatenate([moved_points[1], points, moved_points[-1]], axis=1)
    window_vectors = jnp.concatenate([moved_vectors[1], vectors, moved_vectors[-1]], axis=1)
    leaf_vectors = vectors.reshape(vec_count, leaves, leaf_size)
    coefficients = jnp.einsum(
        "vlp,lrp->lvr", leaf_vectors, leaf_basis, preferred_element_type=jnp.float32
    ).astype(jnp.bfloat16)
    flat_coef = coefficients.reshape(leaves, vec_count * rank)
    pieces = {0: flat_coef}
    shift_list = list(range(REACH, 0, -1)) + list(range(-1, -REACH - 1, -1))
    for shift_by in shift_list:
        pieces[shift_by] = from_behind(flat_coef, ("sect", "dev"), shift_by)
    transfers = local_transfer.reshape(2 * leaves - 2, rank, rank)
    up_chain = [coefficients]
    for tree_level in range(levels):
        level_width = leaves >> tree_level
        slot_start = 2 * leaves - 2 * level_width
        product = batched(up_chain[-1], transfers[slot_start : slot_start + level_width])
        up_chain.append((product[0::2] + product[1::2]).astype(jnp.bfloat16))
    device_all = lax.all_gather(up_chain[-1], ("sect", "dev"), axis=0, tiled=True)
    own_up = upper_transfer.reshape(2, rank, rank)
    own_blocks = upper_couple.reshape(2, 3, rank, rank)
    heap_top = jnp.concatenate([jnp.zeros_like(device_all), device_all], axis=0)
    for up_round in range(top_levels):
        kids = lax.dynamic_slice_in_dim(heap_top, 2 * my_index, 2, 0)
        product = batched(kids, own_up)
        mine_new = (product[0:1] + product[1:2]).astype(jnp.bfloat16)
        fresh = lax.all_gather(mine_new, ("sect", "dev"), axis=0, tiled=True)
        heap_top = jnp.concatenate([fresh, heap_top[devices:]], axis=0)
    power = jnp.int32(1)
    for bit_index in range(1, top_levels):
        power = jnp.where(my_index >= 1 << bit_index, jnp.int32(1 << bit_index), power)
    kid_width = 2 * power
    heap_down = jnp.zeros_like(heap_top)
    for down_round in range(top_levels):
        parent = lax.dynamic_slice_in_dim(heap_down, my_index, 1, 0)
        update = batched_back(jnp.concatenate([parent, parent], axis=0), own_up)
        child_terms = []
        for child_slot in range(2):
            child_pos = 2 * my_index + child_slot - kid_width
            offsets_here = odd_offsets if child_slot == 1 else even_offsets
            summed = update[child_slot]
            for slot_index in range(3):
                partner = child_pos + offsets_here[slot_index]
                in_range = (partner >= 0) & (partner < kid_width)
                heap_place = jnp.clip(kid_width + partner, 0, 2 * devices - 1)
                source = lax.dynamic_slice_in_dim(heap_top, heap_place, 1, 0)[0]
                product = jnp.dot(
                    source, own_blocks[child_slot, slot_index], preferred_element_type=jnp.float32
                )
                summed = summed + jnp.where(in_range, product, 0.0)
            child_terms.append(summed)
        children = jnp.stack(child_terms)
        children = jnp.where(my_index == 0, 0.0, children).astype(jnp.bfloat16)
        heap_down = lax.all_gather(children, ("sect", "dev"), axis=0, tiled=True)
    device_down = lax.dynamic_slice_in_dim(heap_down, devices + my_index, 1, 0)
    ordered = [pieces[shift_by] for shift_by in range(REACH, -REACH - 1, -1)]
    far_window = jnp.concatenate(ordered, axis=0)
    local_ids = couple_list - (my_index - REACH) * leaves
    partners = jnp.take(far_window, local_ids.reshape(-1), axis=0).reshape(
        leaves, couple_slots, vec_count, rank
    )
    couple_sum = jnp.einsum(
        "lsvr,lsrt->lvt",
        partners,
        couple_block.reshape(leaves, couple_slots, rank, rank),
        preferred_element_type=jnp.float32,
    )
    parent = device_down
    for tree_level in range(levels - 1, -1, -1):
        level_width = leaves >> tree_level
        slot_start = 2 * leaves - 2 * level_width
        update = batched_back(
            jnp.repeat(parent, 2, axis=0), transfers[slot_start : slot_start + level_width]
        )
        if tree_level == 0:
            update = update + couple_sum
        parent = update.astype(jnp.bfloat16)
    far_field = jnp.einsum("lvr,lrp->vlp", parent, leaf_basis, preferred_element_type=jnp.float32)
    kernel_scale = 1.0 / math.sqrt(leaf_size * (near_slots + 1))
    own_points = points.reshape(3, leaves, leaf_size)
    point_window = window_points.reshape(3, 3 * leaves, leaf_size)
    vector_window = window_vectors.reshape(vec_count, 3 * leaves, leaf_size)
    self_term = near_product(leaf_vectors, kernel_block(own_points, own_points, kernel_scale))
    local_near = near_list - (my_index - 1) * leaves

    def add_slot(slot_index, running):
        column = lax.dynamic_slice_in_dim(local_near, slot_index, 1, 1)[:, 0]
        source_points = jnp.take(point_window, column, axis=1)
        source_vectors = jnp.take(vector_window, column, axis=1)
        kernel = kernel_block(source_points, own_points, kernel_scale)
        update = near_product(source_vectors, kernel)
        live_slot = (slot_index < near_count)[None, :, None]
        return running + jnp.where(live_slot, update, 0.0)

    near_field = lax.fori_loop(0, near_slots, add_slot, self_term)
    return (far_field + near_field).reshape(vec_count, leaves * leaf_size)


def solution(mesh):
    placed = (
        P(None, ("sect", "dev")),
        P(None, ("sect", "dev")),
        P(("sect", "dev"), None),
        P(("sect", "dev")),
        P(("sect", "dev"), None),
        P(("sect", "dev"), None, None),
        P(("sect", "dev"), None, None),
        P(("sect", "dev"), None, None),
        P(("sect", "dev"), None),
        P(("sect", "dev"), None, None),
    )
    return jax.shard_map(
        shards, mesh=mesh, in_specs=placed, out_specs=P(None, ("sect", "dev")), check_vma=False
    )
```

profile of v0, /device:TPU:1, one launch (start us, length us, event | category | flops | bytes accessed | tf_op | source)
XLA Modules:
  0.0 1252.3 jit_solution(6279758842215728827)
XLA Ops:
  39.0 62.4 %all_gather.45 = bf16[128,8,64]{2,1,0:T(8,128)(2,1)S(1)} all-gather(bf16[1,8,64]{2,1,0:T(8,128)(2,1)S(1)} %fusion.120), channel_id=1, replica_groups=mesh['sect'=8,'dev'=16] {'sect','dev'}, dimensions={0}, use_global_device_ids=true | all-gather | bytes 132096 | tf_op jit(solution)/shard_map/all_gather | solution.py:87
  114.2 59.4 %all_gather.46 = bf16[128,8,64]{2,1,0:T(8,128)(2,1)S(1)} all-gather(bf16[1,8,64]{2,1,0:T(8,128)(2,1)S(1)} %fusion.119), channel_id=1, replica_groups=mesh['sect'=8,'dev'=16] {'sect','dev'}, dimensions={0}, use_global_device_ids=true | all-gather | bytes 132096 | tf_op jit(solution)/shard_map/all_gather | solution.py:95
  173.7 59.4 %all_gather.47 = bf16[128,8,64]{2,1,0:T(8,128)(2,1)S(1)} all-gather(bf16[1,8,64]{2,1,0:T(8,128)(2,1)S(1)} %fusion.118), channel_id=1, replica_groups=mesh['sect'=8,'dev'=16] {'sect','dev'}, dimensions={0}, use_global_device_ids=true | all-gather | bytes 132096 | tf_op jit(solution)/shard_map/all_gather | solution.py:95
  233.2 59.4 %all_gather.48 = bf16[128,8,64]{2,1,0:T(8,128)(2,1)S(1)} all-gather(bf16[1,8,64]{2,1,0:T(8,128)(2,1)S(1)} %fusion.117), channel_id=1, replica_groups=mesh['sect'=8,'dev'=16] {'sect','dev'}, dimensions={0}, use_global_device_ids=true | all-gather | bytes 132096 | tf_op jit(solution)/shard_map/all_gather | solution.py:95
  292.7 59.4 %all_gather.49 = bf16[128,8,64]{2,1,0:T(8,128)(2,1)S(1)} all-gather(bf16[1,8,64]{2,1,0:T(8,128)(2,1)S(1)} %fusion.116), channel_id=1, replica_groups=mesh['sect'=8,'dev'=16] {'sect','dev'}, dimensions={0}, use_global_device_ids=true | all-gather | bytes 132096 | tf_op jit(solution)/shard_map/all_gather | solution.py:95
  352.3 59.4 %all_gather.50 = bf16[128,8,64]{2,1,0:T(8,128)(2,1)S(1)} all-gather(bf16[1,8,64]{2,1,0:T(8,128)(2,1)S(1)} %fusion.115), channel_id=1, replica_groups=mesh['sect'=8,'dev'=16] {'sect','dev'}, dimensions={0}, use_global_device_ids=true | all-gather | bytes 132096 | tf_op jit(solution)/shard_map/all_gather | solution.py:95
  411.8 59.4 %all_gather.51 = bf16[128,8,64]{2,1,0:T(8,128)(2,1)S(1)} all-gather(bf16[1,8,64]{2,1,0:T(8,128)(2,1)S(1)} %fusion.114), channel_id=1, replica_groups=mesh['sect'=8,'dev'=16] {'sect','dev'}, dimensions={0}, use_global_device_ids=true | all-gather | bytes 132096 | tf_op jit(solution)/shard_map/all_gather | solution.py:95
  471.3 59.4 %all_gather.52 = bf16[128,8,64]{2,1,0:T(8,128)(2,1)S(1)} all-gather(bf16[1,8,64]{2,1,0:T(8,128)(2,1)S(1)} %fusion.113), channel_id=1, replica_groups=mesh['sect'=8,'dev'=16] {'sect','dev'}, dimensions={0}, use_global_device_ids=true | all-gather | bytes 132096 | tf_op jit(solution)/shard_map/all_gather | solution.py:95
  537.9 58.8 %all_gather.53 = bf16[256,8,64]{2,1,0:T(8,128)(2,1)} all-gather(bf16[2,8,64]{2,1,0:T(8,128)(2,1)S(1)} %fusion.34), channel_id=1, replica_groups=mesh['sect'=8,'dev'=16] {'sect','dev'}, dimensions={0}, use_global_device_ids=true | all-gather | bytes 264192 | tf_op jit(solution)/shard_map/all_gather | solution.py:122
  597.5 55.1 %all_gather.54 = bf16[256,8,64]{2,1,0:T(8,128)(2,1)S(1)} all-gather(bf16[2,8,64]{2,1,0:T(8,128)(2,1)S(1)} %fusion.35), channel_id=1, replica_groups=mesh['sect'=8,'dev'=16] {'sect','dev'}, dimensions={0}, use_global_device_ids=true | all-gather | bytes 264192 | tf_op jit(solution)/shard_map/all_gather | solution.py:122
  652.8 55.1 %all_gather.55 = bf16[256,8,64]{2,1,0:T(8,128)(2,1)S(1)} all-gather(bf16[2,8,64]{2,1,0:T(8,128)(2,1)S(1)} %fusion.36), channel_id=1, replica_groups=mesh['sect'=8,'dev'=16] {'sect','dev'}, dimensions={0}, use_global_device_ids=true | all-gather | bytes 264192 | tf_op jit(solution)/shard_map/all_gather | solution.py:122
  708.0 55.3 %all_gather.56 = bf16[256,8,64]{2,1,0:T(8,128)(2,1)S(1)} all-gather(bf16[2,8,64]{2,1,0:T(8,128)(2,1)S(1)} %fusion.37), channel_id=1, replica_groups=mesh['sect'=8,'dev'=16] {'sect','dev'}, dimensions={0}, use_global_device_ids=true | all-gather | bytes 264192 | tf_op jit(solution)/shard_map/all_gather | solution.py:122
  763.5 55.1 %all_gather.57 = bf16[256,8,64]{2,1,0:T(8,128)(2,1)S(1)} all-gather(bf16[2,8,64]{2,1,0:T(8,128)(2,1)S(1)} %fusion.38), channel_id=1, replica_groups=mesh['sect'=8,'dev'=16] {'sect','dev'}, dimensions={0}, use_global_device_ids=true | all-gather | bytes 264192 | tf_op jit(solution)/shard_map/all_gather | solution.py:122
  818.8 55.1 %all_gather.58 = bf16[256,8,64]{2,1,0:T(8,128)(2,1)S(1)} all-gather(bf16[2,8,64]{2,1,0:T(8,128)(2,1)S(1)} %fusion.39), channel_id=1, replica_groups=mesh['sect'=8,'dev'=16] {'sect','dev'}, dimensions={0}, use_global_device_ids=true | all-gather | bytes 264192 | tf_op jit(solution)/shard_map/all_gather | solution.py:122
  874.1 58.8 %all_gather.59 = bf16[256,8,64]{2,1,0:T(8,128)(2,1)} all-gather(bf16[2,8,64]{2,1,0:T(8,128)(2,1)S(1)} %fusion.40), channel_id=1, replica_groups=mesh['sect'=8,'dev'=16] {'sect','dev'}, dimensions={0}, use_global_device_ids=true | all-gather | bytes 264192 | tf_op jit(solution)/shard_map/all_gather | solution.py:122
  949.5 23.6 %reshape.139 = bf16[64,16,64,64]{3,2,1,0:T(8,128)(2,1)} reshape(bf16[64,16,4096]{2,1,0:T(8,128)(2,1)} %param.19) | data formatting | bytes 16777216 | tf_op jit(solution)/shard_map/reshape | solution.py:133
  999.5 243.4 %while.13 = (s32[]{:T(128)}, f32[8,64,256]{2,0,1:T(8,128)}, s32[64]{0:T(128)S(1)}, s32[64,16]{0,1:T(8,128)S(1)}, f32[3,192,256]{2,0,1:T(4,128)}, /*index=5*/f32[...) while((s32[]{:T(128)}, f32[8,64,256]{2,0,1:T(8,128)}, s32[64]{0:T(128)S(1)}, ...), condition=%wide.region_1.2_spmd, body=%wide.region_0.1_spmd.sunk | while | flops 113690048 | bytes 10491869 | solution.py:163
  1003.2 11.5 fusion.228
  1018.4 11.5 fusion.228
  1033.6 11.5 fusion.228
  1048.9 11.5 fusion.228
  1064.1 11.5 fusion.228
  1079.3 11.5 fusion.228
  1094.5 11.5 fusion.228
  1109.7 11.5 fusion.228
  1124.9 11.5 fusion.228
  1140.1 11.5 fusion.228
  1155.3 11.5 fusion.228
  1170.5 11.5 fusion.228
  1185.8 11.5 fusion.228
  1201.0 11.5 fusion.228
  1216.2 11.5 fusion.228
  (349 shorter events, 182.7 us)
Async XLA Ops:
  0.0 1.6 copy-start
  3.2 28.3 %copy-start.5 = (bf16[64,8,64]{2,1,0:T(8,128)(2,1)}, bf16[64,8,64]{2,1,0:T(8,128)(2,1)S(1)}, u32[]{:S(2)}) copy-start(bf16[64,8,64]{2,1,0:T(8,128)(2,1)S(1)} %convolution_convert_fusion) | copy-start | bytes 196612
  4.0 982.6 %collective-permute-start.3 = (bf16[64,512]{1,0:T(8,128)(2,1)}, bf16[64,512]{1,0:T(8,128)(2,1)}, u32[]{:S(2)}, u32[]{:S(2)}) collective-permute-start(bf16[64,512]{1,0:T(8,128)(2,1)} %reshape.137), channel_id=1, source_target_pairs={{2,0},{3,1},{4,2},{5,3},{6,4},{7,5},{8,6},{9,7},{10,8},{11,9},{12,... | collective-permute-start | bytes 196616 | tf_op jit(solution)/shard_map/ppermute | solution.py:19
  12.4 970.0 %collective-permute-start.2 = (bf16[64,512]{1,0:T(8,128)(2,1)}, bf16[64,512]{1,0:T(8,128)(2,1)}, u32[]{:S(2)}, u32[]{:S(2)}) collective-permute-start(bf16[64,512]{1,0:T(8,128)(2,1)} %reshape.137), channel_id=1, source_target_pairs={{1,0},{2,1},{3,2},{4,3},{5,4},{6,5},{7,6},{8,7},{9,8},{10,9},{11,1... | collective-permute-start | bytes 196616 | tf_op jit(solution)/shard_map/ppermute | solution.py:19
  15.3 963.4 %collective-permute-start.1 = (bf16[64,512]{1,0:T(8,128)(2,1)}, bf16[64,512]{1,0:T(8,128)(2,1)}, u32[]{:S(2)}, u32[]{:S(2)}) collective-permute-start(bf16[64,512]{1,0:T(8,128)(2,1)} %reshape.137), channel_id=1, source_target_pairs={{0,1},{1,2},{2,3},{3,4},{4,5},{5,6},{6,7},{7,8},{8,9},{9,10},{10,1... | collective-permute-start | bytes 196616 | tf_op jit(solution)/shard_map/ppermute | solution.py:19
  17.7 955.4 %collective-permute-start = (bf16[64,512]{1,0:T(8,128)(2,1)}, bf16[64,512]{1,0:T(8,128)(2,1)}, u32[]{:S(2)}, u32[]{:S(2)}) collective-permute-start(bf16[64,512]{1,0:T(8,128)(2,1)} %reshape.137), channel_id=1, source_target_pairs={{0,2},{1,3},{2,4},{3,5},{4,6},{5,7},{6,8},{7,9},{8,10},{9,11},{10,... | collective-permute-start | bytes 196616 | tf_op jit(solution)/shard_map/ppermute | solution.py:19
  20.3 978.0 %collective-permute-start.6 = (bf16[8,16384]{1,0:T(8,128)(2,1)}, bf16[8,16384]{1,0:T(8,128)(2,1)}, u32[]{:S(2)}, u32[]{:S(2)}) collective-permute-start(bf16[8,16384]{1,0:T(8,128)(2,1)} %param.13), channel_id=1, source_target_pairs={{0,1},{1,2},{2,3},{3,4},{4,5},{5,6},{6,7},{7,8},{8,9},{9,10},{10,1... | collective-permute-start | bytes 786440 | tf_op jit(solution)/shard_map/ppermute | solution.py:19
  31.5 7.5 copy-start.3
  939.6 9.7 copy-start.7
  939.6 9.7 copy-start.8
  939.6 9.8 copy-start.4
  949.3 23.8 %copy-start.6 = (bf16[8,16384]{1,0:T(8,128)(2,1)S(1)}, bf16[8,16384]{1,0:T(8,128)(2,1)}, u32[]{:S(2)}) copy-start(bf16[8,16384]{1,0:T(8,128)(2,1)} %param.13) | copy-start | bytes 786436
  949.5 50.0 %copy-start.9 = (s32[64]{0:T(128)S(1)}, s32[64]{0:T(128)}, u32[]{:S(2)}) copy-start(s32[64]{0:T(128)} %param.15) | copy-start | bytes 772
  973.1 25.3 %collective-permute-start.7 = (bf16[8,16384]{1,0:T(8,128)(2,1)S(1)}, bf16[8,16384]{1,0:T(8,128)(2,1)}, u32[]{:S(2)}, u32[]{:S(2)}) collective-permute-start(bf16[8,16384]{1,0:T(8,128)(2,1)S(1)} %copy-done.6), channel_id=1, source_target_pairs={{1,0},{2,1},{3,2},{4,3},{5,4},{6,5},{7,6},{8,7},{9,8},{10,9},{11,1... | collective-permute-start | bytes 786440 | tf_op jit(solution)/shard_map/ppermute | solution.py:19
  978.7 17.6 %collective-permute-start.5 = (f32[3,16384]{1,0:T(4,128)S(1)}, f32[3,16384]{1,0:T(4,128)S(1)}, u32[]{:S(2)}, u32[]{:S(2)}) collective-permute-start(f32[3,16384]{1,0:T(4,128)S(1)} %copy-done.4), channel_id=1, source_target_pairs={{1,0},{2,1},{3,2},{4,3},{5,4},{6,5},{7,6},{8,7},{9,8},{10,9},{11,1... | collective-permute-start | bytes 589832 | tf_op jit(solution)/shard_map/ppermute | solution.py:19
  982.3 14.0 %collective-permute-start.4 = (f32[3,16384]{1,0:T(4,128)S(1)}, f32[3,16384]{1,0:T(4,128)}, u32[]{:S(2)}, u32[]{:S(2)}) collective-permute-start(f32[3,16384]{1,0:T(4,128)S(1)} %copy-done.4), channel_id=1, source_target_pairs={{0,1},{1,2},{2,3},{3,4},{4,5},{5,6},{6,7},{7,8},{8,9},{9,10},{10,1... | collective-permute-start | bytes 589832 | tf_op jit(solution)/shard_map/ppermute | solution.py:19
  1003.2 11.5 copy-start.2
  1018.4 11.5 copy-start.2
  1033.6 11.5 copy-start.2
  1048.8 11.5 copy-start.2
  1064.1 11.5 copy-start.2
  1079.3 11.5 copy-start.2
  1094.5 11.5 copy-start.2
  1109.7 11.5 copy-start.2
  1124.9 11.5 copy-start.2
  1140.1 11.5 copy-start.2
  1155.3 11.5 copy-start.2
  1170.5 11.5 copy-start.2
  1185.8 11.5 copy-start.2
  1201.0 11.5 copy-start.2
  1216.2 11.5 copy-start.2
  1231.4 11.5 copy-start.2
  (16 other events, 14.0 us)
where the time goes:
time: 1260 us; the launch traced here: 1250 us
  blocking collectives  871 us (69%)
  matrix products  222 us (18%)
  local copies, waits for them, and re-layouts  120 us (10%)
  starting transfers between devices  28.3 us (2%)
    all_gather x7, blocking collectives, shards(): fresh = lax.all_gather(mine_new, ('sect', 'dev'), axis=0, tiled=True)  416 us
    all_gather x7, blocking collectives, shards(): heap_down = lax.all_gather(children, ('sect', 'dev'), axis=0, tiled=True)  393 us
    dot_general x17, matrix products, near_product(): jnp.einsum('vnq,nqp->vnp', source_vectors, kernel, preferred_element_type...  194 us
    all_gather x1, blocking collectives, shards(): lax.all_gather(up_chain[-1], ('sect', 'dev'), axis=0, tiled=True)  62.4 us
    gather x16, local copies, waits for them, and re-layouts, add_slot(): source_points = jnp.take(point_window, column, axis=1)  29.7 us
    ppermute x8, starting transfers between devices, from_behind(): return lax.ppermute(block, axis, route)  28.3 us
  transfers between devices with their start and end apart: 8, of which 0 were waited for; matrix products, arithmetic and copies ran while one was open for 8% of the time, Pallas kernels for 0%

commit v1 on v0

v1 whole, which is shorter than its diff:
```python
import functools
import math

import jax
import jax.numpy as jnp
from jax import lax
from jax.experimental import pallas as pl
from jax.experimental.pallas import tpu as pltpu
from jax.sharding import PartitionSpec as P

REACH = 2
AXES = ("sect", "dev")
MESH = pl.DeviceIdType.MESH
NT = (((1,), (1,)), ((), ()))
f32 = jnp.float32
bf16 = jnp.bfloat16

soft_sq = 0.0025
unit = 256.0


def dot(a, b):
    return jnp.dot(a, b, preferred_element_type=f32)


def dot_nt(a, b):
    return lax.dot_general(a, b, NT, preferred_element_type=f32)


def pieces(x):
    first = x.astype(bf16).astype(f32)
    return first, (x - first).astype(bf16).astype(f32)


def features(packed):
    coords = packed.astype(f32)[8:]
    coords = coords + pltpu.roll(coords, 4, 0)
    row = lax.broadcasted_iota(jnp.int32, coords.shape, 0)
    coords = jnp.where(row < 3, coords, 0.0)
    a, b = pieces(coords)
    kept = a + b
    norm = jnp.sum(kept * kept, axis=0, keepdims=True) + 0.5 * soft_sq * unit * unit
    norm = jnp.broadcast_to(norm, coords.shape)
    coarse = (norm * (1.0 / unit)).astype(bf16).astype(f32)
    fine = norm - coarse * unit
    return row, kept, coarse, fine


def source_side(row, kept, coarse, fine):
    x = jnp.where(row == 3, coarse, kept)
    x = jnp.where(row == 4, fine, x)
    x = jnp.where(row == 5, unit, x)
    x = jnp.where(row == 6, 1.0, x)
    return pieces(x)


def target_side(row, kept, coarse, fine):
    x = jnp.where(row == 3, unit, kept * -2.0)
    x = jnp.where(row == 4, 1.0, x)
    x = jnp.where(row == 5, coarse, x)
    x = jnp.where(row == 6, fine, x)
    return pieces(x)


def tile_of(x):
    wide = jnp.concatenate([x, jnp.zeros_like(x)], axis=1)
    return jnp.concatenate([wide, jnp.zeros_like(wide)], axis=0).astype(bf16)


def body(
    devices,
    per_row,
    near_ref,
    count_ref,
    couple_ids,
    points,
    vectors,
    up_mats,
    up_blocks,
    basis_hbm,
    transfer_hbm,
    couple_hbm,
    out,
    window,
    coef_window,
    kids,
    downs,
    outgoing,
    basis,
    transfer,
    couple,
    src_feat,
    tgt_feat,
    rows_scr,
    coef_scr,
    coef_t,
    gathered,
    couple_sum,
    local_scr,
    load_sem,
    win_send,
    win_recv,
    coef_send,
    coef_recv,
    node_send,
    kid_recv,
    down_send,
    down_recv,
):
    leaves, rank, leaf_size = basis.shape
    slots = near_ref.shape[1]
    npts = leaves * leaf_size
    half = devices // 2
    me = lax.axis_index(AXES[0]) * per_row + lax.axis_index(AXES[1])

    def at(d):
        return (lax.div(d, per_row), lax.rem(d, per_row))

    loads = [
        pltpu.make_async_copy(basis_hbm, basis, load_sem.at[0]),
        pltpu.make_async_copy(transfer_hbm, transfer, load_sem.at[1]),
        pltpu.make_async_copy(couple_hbm, couple, load_sem.at[2]),
    ]
    for load in loads:
        load.start()

    kids[...] = jnp.zeros_like(kids)
    downs[...] = jnp.zeros_like(downs)

    width = jnp.int32(1)
    depth = jnp.int32(0)
    for bit in range(1, devices.bit_length() - 1):
        width = jnp.where(me >= 1 << bit, jnp.int32(1 << bit), width)
        depth = jnp.where(me >= 1 << bit, jnp.int32(bit), depth)
    inner = me >= 1
    below = me >= 2
    child = lax.rem(me, 2)
    leaf_parent = half + lax.div(me, 2)
    inner_parent = lax.div(me, 2)
    inner_low = lax.div(width, 2)

    def kid_device(parent, which):
        heap = 2 * parent + which
        return jnp.where(heap >= devices, heap - devices, heap)

    leaf_targets = [
        (leaf_parent, leaf_parent >= 0, 2 + child),
        (leaf_parent - 1, leaf_parent - 1 >= half, 4 + child),
        (leaf_parent + 1, leaf_parent + 1 < devices, child),
    ]
    inner_targets = [
        (inner_parent, below, 2 + child),
        (inner_parent - 1, below & (inner_parent - 1 >= inner_low), 4 + child),
        (inner_parent + 1, below & (inner_parent + 1 < 2 * inner_low), child),
    ]
    has_left = inner & (me - 1 >= width)
    has_right = inner & (me + 1 < 2 * width)
    relations = [(d, c) for d, c, _ in leaf_targets + inner_targets]
    for which in range(2):
        relations.append((kid_device(me, which), inner))
        relations.append((kid_device(me - 1, which), has_left))
        relations.append((kid_device(me + 1, which), has_right))

    barrier = pltpu.get_barrier_semaphore()
    expected = jnp.int32(4)
    ring = {}
    for shift in (1, -1, 2, -2):
        ring[shift] = lax.rem(me + shift + devices, devices)
        pl.semaphore_signal(barrier, inc=1, device_id=at(ring[shift]), device_id_type=MESH)
    for other, cond in relations:
        live = cond & (other != me)
        expected = expected + jnp.where(live, 1, 0)

        @pl.when(live)
        def _():
            pl.semaphore_signal(barrier, inc=1, device_id=at(other), device_id_type=MESH)

    step = 8

    @pl.loop(0, leaves // step)
    def _(i):
        width = step * leaf_size
        lanes = pl.ds(pl.multiple_of(i * width, width), width)
        own = (points[:, lanes] - 0.5) * unit
        rows_scr[...] = jnp.zeros_like(rows_scr)
        rows_scr[0:3] = own
        rows_scr[4:7] = own
        both = rows_scr[...]
        high = both.astype(bf16).astype(f32)
        row = lax.broadcasted_iota(jnp.int32, both.shape, 0)
        split = jnp.where(row < 4, high, both - high)
        packed = jnp.concatenate([vectors[:, lanes].astype(f32), split], axis=0).astype(bf16)
        for k in range(step):
            window[leaves + i * step + k] = packed[:, k * leaf_size : (k + 1) * leaf_size]

    loads[0].wait()
    coef_scr[...] = jnp.zeros_like(coef_scr)
    coefs = []
    for leaf in range(leaves):
        v = vectors[:, pl.ds(leaf * leaf_size, leaf_size)]
        c = dot_nt(v, basis[leaf]).astype(bf16)
        coefs.append(c)
        coef_scr[pl.ds(8 * leaf, 8), 0:rank] = c.astype(f32)
    for v in range(8):
        block = coef_scr[pl.ds(v, leaves, stride=8), :]
        block = jnp.concatenate([block, jnp.zeros_like(block)], axis=0)
        coef_t[pl.ds(v, rank, stride=8), :] = block.T[0:rank]
    coef_window[2] = coef_t[...].astype(bf16)

    pl.semaphore_wait(barrier, expected)

    win_copies = []
    for k, shift in enumerate((1, -1)):
        copy = pltpu.make_async_remote_copy(
            src_ref=window.at[pl.ds(leaves, leaves)],
            dst_ref=window.at[pl.ds((1 - shift) * leaves, leaves)],
            send_sem=win_send.at[k],
            recv_sem=win_recv.at[k],
            device_id=at(ring[shift]),
            device_id_type=MESH,
        )
        copy.start()
        win_copies.append(copy)
    coef_copies = []
    for k, shift in enumerate((1, -1, 2, -2)):
        copy = pltpu.make_async_remote_copy(
            src_ref=coef_window.at[2],
            dst_ref=coef_window.at[2 - shift],
            send_sem=coef_send.at[k],
            recv_sem=coef_recv.at[k],
            device_id=at(ring[shift]),
            device_id_type=MESH,
        )
        copy.start()
        coef_copies.append(copy)

    loads[1].wait()
    level = coefs
    start = 0
    while len(level) > 1:
        above = []
        for i in range(len(level) // 2):
            pair = jnp.concatenate([level[2 * i], level[2 * i + 1]], axis=1)
            mats = transfer[pl.ds((start + 2 * i) * rank, 2 * rank), :]
            above.append(dot(pair, mats).astype(bf16))
        start += len(level)
        level = above

    def node_copy(source, target, slot, sem):
        return pltpu.make_async_remote_copy(
            src_ref=outgoing.at[source],
            dst_ref=kids.at[slot],
            send_sem=node_send.at[sem],
            recv_sem=kid_recv.at[slot],
            device_id=at(target),
            device_id_type=MESH,
        )

    def send_node(source, targets, first_sem):
        for k, (target, cond, slot) in enumerate(targets):

            @pl.when(cond & (target != me))
            def _():
                node_copy(source, target, slot, first_sem + k).start()

            @pl.when(cond & (target == me))
            def _():
                pltpu.make_async_copy(
                    outgoing.at[source], kids.at[slot], kid_recv.at[slot]
                ).start()

    def finish_node(source, targets, first_sem):
        for k, (target, cond, slot) in enumerate(targets):

            @pl.when(cond & (target != me))
            def _():
                node_copy(source, target, slot, first_sem + k).wait_send()

    def wait_kid(slot):
        pltpu.make_async_copy(outgoing.at[0], kids.at[slot], kid_recv.at[slot]).wait()

    def wait_down(slot):
        pltpu.make_async_copy(outgoing.at[0], downs.at[slot], down_recv.at[slot]).wait()

    outgoing[0] = tile_of(level[0].astype(f32))
    send_node(0, leaf_targets, 0)

    def upward():
        wait_kid(2)
        wait_kid(3)
        pair = jnp.concatenate([kids[2][:, 0:rank], kids[3][:, 0:rank]], axis=1)
        top = dot(pair, up_mats[...])
        outgoing[1] = jnp.concatenate([top, jnp.zeros_like(top)], axis=1).astype(bf16)
        send_node(1, inner_targets, 3)

    def down_copy(which):
        target = kid_device(me, which)
        slot = jnp.where(me >= half, 1, 0)
        return target, slot, pltpu.make_async_remote_copy(
            src_ref=outgoing.at[2 + which],
            dst_ref=downs.at[slot],
            send_sem=down_send.at[which],
            recv_sem=down_recv.at[slot],
            device_id=at(target),
            device_id_type=MESH,
        )

    def downward():
        @pl.when(has_left)
        def _():
            wait_kid(0)
            wait_kid(1)

        @pl.when(has_right)
        def _():
            wait_kid(4)
            wait_kid(5)

        @pl.when(below)
        def _():
            wait_down(0)

        update = dot_nt(downs[0][:, 0:rank], up_mats[...])
        a0, a1, c0, c1 = (kids[s][:, 0:rank] for s in (0, 1, 4, 5))
        for which, sources in enumerate(((a0, c0, c1), (a0, a1, c1))):
            blocks = up_blocks[pl.ds(which * 3 * rank, 3 * rank), :]
            term = dot(jnp.concatenate(sources, axis=1), blocks)
            total = update[:, which * rank : (which + 1) * rank] + term
            wide = jnp.concatenate([total, jnp.zeros_like(total)], axis=1)
            outgoing[2 + which] = wide.astype(bf16)
            target, slot, copy = down_copy(which)

            @pl.when(target != me)
            def _():
                copy.start()

            @pl.when(target == me)
            def _():
                pltpu.make_async_copy(
                    outgoing.at[2 + which], downs.at[slot], down_recv.at[slot]
                ).start()

    def build(place, leaf):
        packed = window[place * leaves + leaf]
        parts = features(packed)
        p = source_side(*parts)
        stacked = jnp.concatenate([p[0], p[0], p[1], p[1]], axis=0)
        src_feat[place * leaves + leaf] = stacked.T.astype(bf16)
        return parts

    @pl.loop(0, leaves)
    def _(leaf):
        parts = build(1, leaf)
        q = target_side(*parts)
        stacked = jnp.concatenate([q[0], q[1], q[0], q[1]], axis=0)
        tgt_feat[leaf] = stacked.astype(bf16)

    for copy in win_copies:
        copy.wait_recv()

    @pl.loop(0, leaves)
    def _(leaf):
        build(0, leaf)
        build(2, leaf)

    scale = unit / math.sqrt(leaf_size * (slots + 1))
    levels = devices.bit_length() - 1
    gap = 3
    up_at = jnp.where(inner, 2 + gap * (levels - 1 - depth), -1)
    down_at = jnp.where(inner, 2 + gap * (levels + depth), -1)

    @pl.loop(0, leaves)
    def _(leaf):
        target = tgt_feat[leaf]
        live = count_ref[leaf]
        weights = []
        kernels = []
        for s in range(slots + 1):
            m = leaf + leaves
            if s:
                m = near_ref[leaf, s - 1] - (me - 1) * leaves
                m = jnp.minimum(jnp.maximum(m, 0), 3 * leaves - 1)
            d = dot(src_feat[m], target)
            kernels.append(lax.rsqrt(d).astype(bf16))
            v = window[m]
            if s:
                used = jnp.minimum(jnp.maximum(live - (s - 1), 0), 1).astype(f32)
                v = (v.astype(f32) * used).astype(bf16)
            weights.append(v)
        near = dot(jnp.concatenate(weights, axis=1), jnp.concatenate(kernels, axis=0))
        out[:, pl.ds(pl.multiple_of(leaf * leaf_size, leaf_size), leaf_size)] = near[0:8] * scale

        @pl.when(leaf == up_at)
        def _():
            upward()

        @pl.when(leaf == down_at)
        def _():
            downward()

    for copy in coef_copies:
        copy.wait_recv()
    loads[2].wait()
    places = couple_ids[...] - (me - REACH) * leaves
    spread = lax.div(places, leaves) * 128 + lax.rem(places, leaves)
    total = None
    for k in range(2 * REACH + 1):
        row = lax.broadcasted_iota(jnp.int32, (128, spread.shape[1]), 0) + 128 * k
        chosen = jnp.where(row == spread, 1.0, 0.0).astype(bf16)
        part = dot(coef_window[k], chosen)
        total = part if total is None else total + part
    gathered[...] = total.astype(bf16)

    group = 128 // couple.shape[1]
    chunks = rank * rank // 128

    @pl.loop(0, leaves // group)
    def _(g):
        row = lax.broadcasted_iota(jnp.int32, (128, 128), 0)
        lane = lax.broadcasted_iota(jnp.int32, (128, 128), 1)
        mask = jnp.where(lax.div(row, 16) == lax.div(lane, 16), 1.0, 0.0).astype(bf16)
        lefts = []
        rights = []
        lanes = pl.ds(pl.multiple_of(g * 128, 128), 128)
        for j in range(chunks):
            x = gathered[pl.ds(16 * j, 16), lanes]
            lefts.append(jnp.concatenate([x] * group, axis=0) * mask)
            block = couple[pl.ds(g * group, group), :, pl.ds(128 * j, 128)]
            rights.append(block.reshape(128, 128))
        r = dot(jnp.concatenate(lefts, axis=1), jnp.concatenate(rights, axis=0))
        r = r.reshape(group, 16, 128)
        couple_sum[pl.ds(g * group, group)] = r[:, 0:8, 0:rank] + r[:, 8:16, rank : 2 * rank]

    wait_down(1)
    parents = [downs[1][0:8, 0:rank]]
    while len(parents) < leaves:
        below_here = []
        count = 2 * len(parents)
        start = 2 * leaves - 2 * count
        for i, parent in enumerate(parents):
            mats = transfer[pl.ds((start + 2 * i) * rank, 2 * rank), :]
            both = dot_nt(parent, mats)
            for which in range(2):
                update = both[:, which * rank : (which + 1) * rank]
                if count == leaves:
                    update = update + couple_sum[2 * i + which]
                below_here.append(update.astype(bf16))
        parents = below_here
    for leaf in range(leaves):
        lanes = pl.ds(leaf * leaf_size, leaf_size)
        out[:, lanes] = out[:, lanes] + dot(parents[leaf], basis[leaf])

    for copy in win_copies + coef_copies:
        copy.wait_send()
    finish_node(0, leaf_targets, 0)
    finish_node(1, inner_targets, 3)
    for which in range(2):
        target, slot, copy = down_copy(which)

        @pl.when(inner & (target != me))
        def _():
            copy.wait_send()


def shards(
    points,
    vectors,
    near_list,
    near_count,
    couple_list,
    leaf_basis,
    local_transfer,
    couple_block,
    upper_transfer,
    upper_couple,
):
    devices = lax.axis_size(AXES)
    per_row = lax.axis_size(AXES[1])
    leaves, rank, leaf_size = leaf_basis.shape
    npts = points.shape[1]
    couples = couple_list.shape[1]
    vmem = pl.BlockSpec(memory_space=pltpu.VMEM)
    smem = pl.BlockSpec(memory_space=pltpu.SMEM)
    hbm = pl.BlockSpec(memory_space=pl.ANY)
    dma = pltpu.SemaphoreType.DMA
    call = pl.pallas_call(
        functools.partial(body, devices, per_row),
        out_shape=jax.ShapeDtypeStruct((8, npts), f32),
        in_specs=[smem, smem, vmem, vmem, vmem, vmem, vmem, hbm, hbm, hbm],
        out_specs=vmem,
        scratch_shapes=[
            pltpu.VMEM((3 * leaves, 16, leaf_size), bf16),
            pltpu.VMEM((2 * REACH + 1, 8 * rank, 128), bf16),
            pltpu.VMEM((6, 16, 128), bf16),
            pltpu.VMEM((2, 16, 128), bf16),
            pltpu.VMEM((4, 16, 128), bf16),
            pltpu.VMEM((leaves, rank, leaf_size), bf16),
            pltpu.VMEM(((2 * leaves - 2) * rank, rank), bf16),
            pltpu.VMEM((leaves, couples, rank * rank), bf16),
            pltpu.VMEM((3 * leaves, leaf_size, 32), bf16),
            pltpu.VMEM((leaves, 32, leaf_size), bf16),
            pltpu.VMEM((8, 2048), f32),
            pltpu.VMEM((8 * leaves, 128), f32),
            pltpu.VMEM((8 * rank, 128), f32),
            pltpu.VMEM((8 * rank, leaves * couples), bf16),
            pltpu.VMEM((leaves, 8, rank), f32),
            pltpu.VMEM((leaves, 8, rank), f32),
            dma((3,)),
            dma((2,)),
            dma((2,)),
            dma((4,)),
            dma((4,)),
            dma((6,)),
            dma((6,)),
            dma((2,)),
            dma((2,)),
        ],
        compiler_params=pltpu.CompilerParams(
            collective_id=0, has_side_effects=True, vmem_limit_bytes=56 << 20
        ),
        name="h2_product",
    )
    return call(
        near_list,
        near_count,
        couple_list.reshape(1, leaves * couples),
        points,
        vectors,
        upper_transfer.reshape(2 * rank, rank),
        upper_couple.reshape(6 * rank, rank),
        leaf_basis,
        local_transfer.reshape((2 * leaves - 2) * rank, rank),
        couple_block,
    )


def solution(mesh):
    placed = (
        P(None, AXES),
        P(None, AXES),
        P(AXES, None),
        P(AXES),
        P(AXES, None),
        P(AXES, None, None),
        P(AXES, None, None),
        P(AXES, None, None),
        P(AXES, None),
        P(AXES, None, None),
    )
    return jax.shard_map(
        shards, mesh=mesh, in_specs=placed, out_specs=P(None, AXES), check_vma=False
    )
```

time: 1260 us -> 132 us (0.10)
  blocking collectives: 871 us -> 0 us
  matrix products: 222 us -> 0 us
  Pallas kernels: 0 us -> 118 us
  local copies, waits for them, and re-layouts: 120 us -> 11.9 us
  starting transfers between devices: 28.3 us -> 0 us
    all_gather x15 -> x0, blocking collectives: 871 us -> none  [the longest x7 416 us: shards(): fresh = lax.all_gather(mine_new, ('sect', 'dev'), axis=0, tiled=True)]
    dot_general x51 -> x0, matrix products: 222 us -> none  [the longest x17 194 us: near_product(): jnp.einsum('vnq,nqp->vnp', source_vectors, kernel, preferred_element_type...]
    pallas_call x0 -> x1, Pallas kernels: none -> 118 us  [shards(): call(near_list, near_count, couple_list.reshape(1, leaves * couples), poi...]
    gather x34 -> x0, local copies, waits for them, and re-layouts: 48.1 us -> none  [the longest x16 29.7 us: add_slot(): source_points = jnp.take(point_window, column, axis=1)]
    ppermute x8 -> x0, starting transfers between devices: 28.3 us -> none  [from_behind(): return lax.ppermute(block, axis, route)]
    reshape x5 -> x4, local copies, waits for them, and re-layouts: 27.6 us -> 7.06 us  [the longest x1 4.2 us: shards(): local_transfer.reshape((2 * leaves - 2) * rank, rank)]
    slice x29 -> x0, local copies, waits for them, and re-layouts: 15.7 us -> none  [the longest x12 11 us: shards(): transfers[slot_start:slot_start + level_width]]
    while x80 -> x0, local copies, waits for them, and re-layouts: 13.4 us -> none
  transfers between devices with their start and end apart: 8 -> 0, of which waited for: 0 -> 0; matrix products, arithmetic and copies ran while one was open for 8% -> 0% of each run, Pallas kernels for 0% -> 0%
where the time goes in v1:
time: 132 us; the launch traced here: 130 us
  Pallas kernels  118 us (89%)
  local copies, waits for them, and re-layouts  11.9 us (9%)
    pallas_call x1, Pallas kernels, shards(): call(near_list, near_count, couple_list.reshape(1, leaves * couples), poi...  118 us
    unnamed x4, local copies, waits for them, and re-layouts  4.87 us
    reshape x1, local copies, waits for them, and re-layouts, shards(): local_transfer.reshape((2 * leaves - 2) * rank, rank)  4.2 us

profile of v1, /device:TPU:1, one launch (start us, length us, event | category | flops | bytes accessed | tf_op | source)
XLA Modules:
  0.0 130.3 jit_solution(16997321493116248957)
XLA Ops:
  0.0 1.4 %copy.16.near_ref = s32[64,16]{1,0:T(8,128)} copy(s32[64,16]{0,1:T(8,128)} %param.12) | data formatting | bytes 8192 | tf_op args[2]
  1.4 0.8 copy.14
  2.2 0.7 reshape.12.couple_ids
  2.8 1.4 %reshape.13.up_mats = bf16[128,64]{1,0:T(8,128)(2,1)} reshape(bf16[2,4096]{1,0:T(2,128)(2,1)} %param.18) | data formatting | bytes 32768 | tf_op jit(solution)/shard_map/reshape | solution.py:529
  4.3 0.8 copy.15
  5.1 0.8 reshape.14.up_blocks
  5.9 4.2 %reshape.15.transfer_hbm = bf16[8064,64]{1,0:T(8,128)(2,1)} reshape(bf16[1,126,4096]{2,1,0:T(8,128)(2,1)} %param.16) | data formatting | bytes 2064384 | tf_op jit(solution)/shard_map/reshape | solution.py:532
  10.1 118.4 %h2_product.1 = f32[8,16384]{1,0:T(8,128)} custom-call(s32[64,16]{1,0:T(8,128)} %copy.16.near_ref, s32[64]{0:T(128)} %count_ref.1, s32[1,1024]{1,0:T(1,128)} %reshape.12.couple_ids, f32[3,16384]{1,0:T(4,128)} %points.1, bf16[8,16384]{1,0:T(8,128)(2,1)} %vectors.1, bf16[128,64]{1,0:T(8,128)(2,1)} %reshape.13.up_mats, bf16[384,64]{1,0:T(8,128)(2,1)} %reshape.14.up_blocks, ...), custom_call_target="tpu_custom_call" | custom-call | tf_op jit(solution)/shard_map/h2_product/pallas_call | solution.py:523
  128.5 1.9 %copy.18 = f32[8,16384]{1,0:T(8,128)} copy(f32[8,16384]{1,0:T(8,128)} %h2_product.1) | data formatting | bytes 1048576

commit v2 on v1

--- a/solution.py
+++ b/solution.py
@@ -12,6 +12,7 @@
 AXES = ("sect", "dev")
 MESH = pl.DeviceIdType.MESH
 NT = (((1,), (1,)), ((), ()))
+TN = (((0,), (0,)), ((), ()))
 f32 = jnp.float32
 bf16 = jnp.bfloat16
 
@@ -23,43 +24,44 @@
     return jnp.dot(a, b, preferred_element_type=f32)
 
 
+def dot_tn(a, b):
+    return lax.dot_general(a, b, TN, preferred_element_type=f32)
+
+
 def dot_nt(a, b):
     return lax.dot_general(a, b, NT, preferred_element_type=f32)
 
 
-def pieces(x):
-    first = x.astype(bf16).astype(f32)
-    return first, (x - first).astype(bf16).astype(f32)
-
-
-def features(packed):
-    coords = packed.astype(f32)[8:]
-    coords = coords + pltpu.roll(coords, 4, 0)
-    row = lax.broadcasted_iota(jnp.int32, coords.shape, 0)
-    coords = jnp.where(row < 3, coords, 0.0)
-    a, b = pieces(coords)
-    kept = a + b
-    norm = jnp.sum(kept * kept, axis=0, keepdims=True) + 0.5 * soft_sq * unit * unit
-    norm = jnp.broadcast_to(norm, coords.shape)
-    coarse = (norm * (1.0 / unit)).astype(bf16).astype(f32)
-    fine = norm - coarse * unit
-    return row, kept, coarse, fine
-
-
-def source_side(row, kept, coarse, fine):
-    x = jnp.where(row == 3, coarse, kept)
-    x = jnp.where(row == 4, fine, x)
-    x = jnp.where(row == 5, unit, x)
-    x = jnp.where(row == 6, 1.0, x)
-    return pieces(x)
-
-
-def target_side(row, kept, coarse, fine):
-    x = jnp.where(row == 3, unit, kept * -2.0)
-    x = jnp.where(row == 4, 1.0, x)
-    x = jnp.where(row == 5, coarse, x)
-    x = jnp.where(row == 6, fine, x)
-    return pieces(x)
+def round16(x):
+    return x.astype(bf16).astype(f32)
+
+
+def leaf_rows(own, row):
+    edge = (row & 3) == 3
+    high = round16(own)
+    kept = jnp.where(edge, 0.0, high + round16(own - high))
+    norm = 0.5 * jnp.sum(kept * kept, axis=0, keepdims=True) + 0.5 * soft_sq * unit * unit
+    norm = jnp.broadcast_to(norm, own.shape)
+    source = jnp.where(edge, norm, kept)
+    high = round16(source)
+    source = jnp.where(row < 4, high, source - high)
+    facing = jnp.where(edge, 1.0, kept * -2.0)
+    facing_high = round16(facing)
+    n_one = round16(norm)
+    n_two = round16(norm - n_one)
+    norms = jnp.where(row == 1, n_two, norm - n_one - n_two)
+    norms = jnp.where(row == 0, n_one, jnp.where(row < 3, norms, 0.0))
+    nothing = jnp.zeros_like(own)
+    target = [nothing, facing_high, nothing, facing - facing_high, norms, nothing]
+    return source, jnp.concatenate(target, axis=0)
+
+
+def shuffled(rows, columns, shift):
+    r = lax.broadcasted_iota(jnp.int32, (rows, columns), 0)
+    c = lax.broadcasted_iota(jnp.int32, (rows, columns), 1)
+    half = columns // 2
+    origin = 2 * (c & (half - 1)) + jnp.where(c >= half, 1, 0)
+    return jnp.where(r == origin + shift, 1.0, 0.0).astype(bf16)
 
 
 def tile_of(x):
@@ -87,16 +89,18 @@
     downs,
     outgoing,
     basis,
+    stored,
+    couple,
     transfer,
-    couple,
-    src_feat,
+    upper_scr,
+    wide_scr,
+    upper,
     tgt_feat,
     rows_scr,
     coef_scr,
     coef_t,
     gathered,
     couple_sum,
-    local_scr,
     load_sem,
     win_send,
     win_recv,
@@ -108,7 +112,7 @@
     down_recv,
 ):
     leaves, rank, leaf_size = basis.shape
-    slots = near_ref.shape[1]
+    slots = near_ref.shape[0]
     npts = leaves * leaf_size
     half = devices // 2
     me = lax.axis_index(AXES[0]) * per_row + lax.axis_index(AXES[1])
@@ -118,7 +122,7 @@
 
     loads = [
         pltpu.make_async_copy(basis_hbm, basis, load_sem.at[0]),
-        pltpu.make_async_copy(transfer_hbm, transfer, load_sem.at[1]),
+        pltpu.make_async_copy(transfer_hbm, stored, load_sem.at[1]),
         pltpu.make_async_copy(couple_hbm, couple, load_sem.at[2]),
     ]
     for load in loads:
@@ -179,33 +183,19 @@
 
     @pl.loop(0, leaves // step)
     def _(i):
-        width = step * leaf_size
-        lanes = pl.ds(pl.multiple_of(i * width, width), width)
+        lanes = pl.ds(pl.multiple_of(i * step * leaf_size, step * leaf_size), step * leaf_size)
         own = (points[:, lanes] - 0.5) * unit
         rows_scr[...] = jnp.zeros_like(rows_scr)
         rows_scr[0:3] = own
         rows_scr[4:7] = own
         both = rows_scr[...]
-        high = both.astype(bf16).astype(f32)
-        row = lax.broadcasted_iota(jnp.int32, both.shape, 0)
-        split = jnp.where(row < 4, high, both - high)
-        packed = jnp.concatenate([vectors[:, lanes].astype(f32), split], axis=0).astype(bf16)
+        source, target = leaf_rows(both, lax.broadcasted_iota(jnp.int32, both.shape, 0))
+        packed = jnp.concatenate([vectors[:, lanes].astype(f32), source], axis=0).astype(bf16)
+        target = target.astype(bf16)
         for k in range(step):
-            window[leaves + i * step + k] = packed[:, k * leaf_size : (k + 1) * leaf_size]
-
-    loads[0].wait()
-    coef_scr[...] = jnp.zeros_like(coef_scr)
-    coefs = []
-    for leaf in range(leaves):
-        v = vectors[:, pl.ds(leaf * leaf_size, leaf_size)]
-        c = dot_nt(v, basis[leaf]).astype(bf16)
-        coefs.append(c)
-        coef_scr[pl.ds(8 * leaf, 8), 0:rank] = c.astype(f32)
-    for v in range(8):
-        block = coef_scr[pl.ds(v, leaves, stride=8), :]
-        block = jnp.concatenate([block, jnp.zeros_like(block)], axis=0)
-        coef_t[pl.ds(v, rank, stride=8), :] = block.T[0:rank]
-    coef_window[2] = coef_t[...].astype(bf16)
+            part = slice(k * leaf_size, (k + 1) * leaf_size)
+            window[leaves + i * step + k] = packed[:, part]
+            tgt_feat[i * step + k] = target[:, part]
 
     pl.semaphore_wait(barrier, expected)
 
@@ -221,6 +211,17 @@
         )
         copy.start()
         win_copies.append(copy)
+
+    loads[0].wait()
+    coef_scr[...] = jnp.zeros_like(coef_scr)
+    for leaf in range(leaves):
+        v = vectors[:, pl.ds(leaf * leaf_size, leaf_size)]
+        coef_scr[pl.ds(8 * leaf, 8), 0:rank] = round16(dot_nt(v, basis[leaf]))
+    for v in range(8):
+        block = coef_scr[pl.ds(v, leaves, stride=8), :]
+        block = jnp.concatenate([block, jnp.zeros_like(block)], axis=0)
+        coef_t[pl.ds(v, rank, stride=8), :] = block.T[0:rank]
+    coef_window[2] = coef_t[...].astype(bf16)
     coef_copies = []
     for k, shift in enumerate((1, -1, 2, -2)):
         copy = pltpu.make_async_remote_copy(
@@ -234,15 +235,51 @@
         copy.start()
         coef_copies.append(copy)
 
+    half_rank = rank // 2
+    lower = shuffled(2 * rank, rank, 0)
+    higher = shuffled(2 * rank, rank, rank)
+    upper_scr[0:2] = up_mats[...].astype(f32)
+    for s in range(3):
+        upper_scr[2 + 2 * s : 4 + 2 * s] = up_blocks[s].astype(f32)
+    for j in range(half_rank):
+        wide_scr[pl.ds(j, 8, stride=half_rank), :] = upper_scr[:, pl.ds(128 * j, 128)]
+    natural = wide_scr[0 : 8 * half_rank].astype(bf16)
+    for p, pick in enumerate((lower, higher)):
+        part = dot(natural, pick).astype(bf16)
+        upper[:, pl.ds(half_rank * p, half_rank)] = part.reshape(8, half_rank, rank)
     loads[1].wait()
-    level = coefs
+    nodes = 2 * leaves - 2
+    for j in range(half_rank):
+        for first in range(0, nodes, 16):
+            count = min(16, nodes - first)
+            tile = stored[pl.ds(first, count), pl.ds(128 * j, 128)].astype(f32)
+            for k in range(0, count, 8):
+                some = min(8, count - k)
+                place = pl.ds((first + k) * half_rank + j, some, stride=half_rank)
+                wide_scr[place, :] = tile[k : k + some]
+    group = 14
+
+    @pl.loop(0, nodes // group)
+    def _(i):
+        size = group * half_rank
+        natural = wide_scr[pl.ds(pl.multiple_of(i * size, size), size), :].astype(bf16)
+        for p, pick in enumerate((lower, higher)):
+            part = dot(natural, pick).astype(bf16)
+            part = part.reshape(group, half_rank, rank)
+            transfer[pl.ds(i * group, group), pl.ds(half_rank * p, half_rank)] = part
+
+    def pair_of(node):
+        return transfer[pl.ds(node, 2)].reshape(2 * rank, rank)
+
+    shuffle = shuffled(rank, rank, 0)
+    whole = dot(coef_scr[:, 0:rank].astype(bf16), shuffle)
+    level = [whole[8 * leaf : 8 * leaf + 8] for leaf in range(leaves)]
     start = 0
     while len(level) > 1:
         above = []
         for i in range(len(level) // 2):
-            pair = jnp.concatenate([level[2 * i], level[2 * i + 1]], axis=1)
-            mats = transfer[pl.ds((start + 2 * i) * rank, 2 * rank), :]
-            above.append(dot(pair, mats).astype(bf16))
+            pair = jnp.concatenate([level[2 * i], level[2 * i + 1]], axis=1).astype(bf16)
+            above.append(round16(dot(pair, pair_of(start + 2 * i))))
         start += len(level)
         level = above
 
@@ -282,14 +319,14 @@
     def wait_down(slot):
         pltpu.make_async_copy(outgoing.at[0], downs.at[slot], down_recv.at[slot]).wait()
 
-    outgoing[0] = tile_of(level[0].astype(f32))
+    outgoing[0] = tile_of(level[0])
     send_node(0, leaf_targets, 0)
 
     def upward():
         wait_kid(2)
         wait_kid(3)
         pair = jnp.concatenate([kids[2][:, 0:rank], kids[3][:, 0:rank]], axis=1)
-        top = dot(pair, up_mats[...])
+        top = dot(pair, upper[0:2].reshape(2 * rank, rank))
         outgoing[1] = jnp.concatenate([top, jnp.zeros_like(top)], axis=1).astype(bf16)
         send_node(1, inner_targets, 3)
 
@@ -320,10 +357,10 @@
         def _():
             wait_down(0)
 
-        update = dot_nt(downs[0][:, 0:rank], up_mats[...])
+        update = dot_nt(downs[0][:, 0:rank], upper[0:2].reshape(2 * rank, rank))
         a0, a1, c0, c1 = (kids[s][:, 0:rank] for s in (0, 1, 4, 5))
         for which, sources in enumerate(((a0, c0, c1), (a0, a1, c1))):
-            blocks = up_blocks[pl.ds(which * 3 * rank, 3 * rank), :]
+            blocks = jnp.concatenate([upper[2 + 2 * k + which] for k in range(3)], axis=0)
             term = dot(jnp.concatenate(sources, axis=1), blocks)
             total = update[:, which * rank : (which + 1) * rank] + term
             wide = jnp.concatenate([total, jnp.zeros_like(total)], axis=1)
@@ -340,69 +377,21 @@
                     outgoing.at[2 + which], downs.at[slot], down_recv.at[slot]
                 ).start()
 
-    def build(place, leaf):
-        packed = window[place * leaves + leaf]
-        parts = features(packed)
-        p = source_side(*parts)
-        stacked = jnp.concatenate([p[0], p[0], p[1], p[1]], axis=0)
-        src_feat[place * leaves + leaf] = stacked.T.astype(bf16)
-        return parts
-
-    @pl.loop(0, leaves)
-    def _(leaf):
-        parts = build(1, leaf)
-        q = target_side(*parts)
-        stacked = jnp.concatenate([q[0], q[1], q[0], q[1]], axis=0)
-        tgt_feat[leaf] = stacked.astype(bf16)
-
-    for copy in win_copies:
-        copy.wait_recv()
-
-    @pl.loop(0, leaves)
-    def _(leaf):
-        build(0, leaf)
-        build(2, leaf)
-
-    scale = unit / math.sqrt(leaf_size * (slots + 1))
-    levels = devices.bit_length() - 1
-    gap = 3
-    up_at = jnp.where(inner, 2 + gap * (levels - 1 - depth), -1)
-    down_at = jnp.where(inner, 2 + gap * (levels + depth), -1)
-
-    @pl.loop(0, leaves)
-    def _(leaf):
-        target = tgt_feat[leaf]
-        live = count_ref[leaf]
-        weights = []
-        kernels = []
-        for s in range(slots + 1):
-            m = leaf + leaves
-            if s:
-                m = near_ref[leaf, s - 1] - (me - 1) * leaves
-                m = jnp.minimum(jnp.maximum(m, 0), 3 * leaves - 1)
-            d = dot(src_feat[m], target)
-            kernels.append(lax.rsqrt(d).astype(bf16))
-            v = window[m]
-            if s:
-                used = jnp.minimum(jnp.maximum(live - (s - 1), 0), 1).astype(f32)
-                v = (v.astype(f32) * used).astype(bf16)
-            weights.append(v)
-        near = dot(jnp.concatenate(weights, axis=1), jnp.concatenate(kernels, axis=0))
-        out[:, pl.ds(pl.multiple_of(leaf * leaf_size, leaf_size), leaf_size)] = near[0:8] * scale
-
-        @pl.when(leaf == up_at)
-        def _():
-            upward()
-
-        @pl.when(leaf == down_at)
-        def _():
-            downward()
-
     for copy in coef_copies:
         copy.wait_recv()
-    loads[2].wait()
+    couples = couple.shape[1]
+    columns = leaves * couples
     places = couple_ids[...] - (me - REACH) * leaves
-    spread = lax.div(places, leaves) * 128 + lax.rem(places, leaves)
+    owner = lax.div(places, leaves)
+    both = jnp.concatenate([owner, places - owner * leaves], axis=0).astype(bf16)
+    row = lax.broadcasted_iota(jnp.int32, (leaves, columns), 0)
+    lane = lax.broadcasted_iota(jnp.int32, (leaves, columns), 1)
+    spread = dot(both, jnp.where(row == lax.div(lane, couples), 1.0, 0.0).astype(bf16))
+    spread = spread[0:couples] * 128.0 + spread[couples:]
+    row = lax.broadcasted_iota(jnp.int32, (couples, columns), 0)
+    lane = lax.broadcasted_iota(jnp.int32, (couples, columns), 1)
+    spread = jnp.where(row == lax.rem(lane, couples), spread, 0.0)
+    spread = jnp.sum(spread, axis=0, keepdims=True).astype(jnp.int32)
     total = None
     for k in range(2 * REACH + 1):
         row = lax.broadcasted_iota(jnp.int32, (128, spread.shape[1]), 0) + 128 * k
@@ -411,7 +400,8 @@
         total = part if total is None else total + part
     gathered[...] = total.astype(bf16)
 
-    group = 128 // couple.shape[1]
+    group = 128 // couples
+    loads[2].wait()
     chunks = rank * rank // 128
 
     @pl.loop(0, leaves // group)
@@ -431,6 +421,50 @@
         r = r.reshape(group, 16, 128)
         couple_sum[pl.ds(g * group, group)] = r[:, 0:8, 0:rank] + r[:, 8:16, rank : 2 * rank]
 
+    flat = couple_sum[...].reshape(8 * leaves, rank)
+    coarse = flat.astype(bf16)
+    flat = dot(coarse, shuffle) + dot((flat - coarse.astype(f32)).astype(bf16), shuffle)
+    couple_sum[...] = flat.reshape(leaves, 8, rank)
+
+    for copy in win_copies:
+        copy.wait_recv()
+
+    scale = unit / math.sqrt(leaf_size * (slots + 1))
+    levels = devices.bit_length() - 1
+    gap = 3
+    up_at = jnp.where(inner, 2 + gap * (levels - 1 - depth), -1)
+    down_at = jnp.where(inner, 2 + gap * (levels + depth), -1)
+
+    @pl.loop(0, leaves)
+    def _(leaf):
+        target = tgt_feat[leaf]
+        live = count_ref[leaf]
+        ones = jnp.ones((16, leaf_size), bf16)
+        weights = []
+        kernels = []
+        for s in range(slots + 1):
+            m = leaf + leaves
+            if s:
+                m = near_ref[s - 1, leaf] - (me - 1) * leaves
+                m = jnp.minimum(jnp.maximum(m, 0), 3 * leaves - 1)
+            v = window[m]
+            d = dot_tn(jnp.concatenate([v, v, ones], axis=0), target)
+            kernels.append(lax.rsqrt(d).astype(bf16))
+            if s:
+                used = jnp.minimum(jnp.maximum(live - (s - 1), 0), 1).astype(f32)
+                v = (v.astype(f32) * used).astype(bf16)
+            weights.append(v)
+        near = dot(jnp.concatenate(weights, axis=1), jnp.concatenate(kernels, axis=0))
+        out[:, pl.ds(pl.multiple_of(leaf * leaf_size, leaf_size), leaf_size)] = near[0:8] * scale
+
+        @pl.when(leaf == up_at)
+        def _():
+            upward()
+
+        @pl.when(leaf == down_at)
+        def _():
+            downward()
+
     wait_down(1)
     parents = [downs[1][0:8, 0:rank]]
     while len(parents) < leaves:
@@ -438,17 +472,19 @@
         count = 2 * len(parents)
         start = 2 * leaves - 2 * count
         for i, parent in enumerate(parents):
-            mats = transfer[pl.ds((start + 2 * i) * rank, 2 * rank), :]
-            both = dot_nt(parent, mats)
+            both = dot_nt(parent, pair_of(start + 2 * i))
             for which in range(2):
                 update = both[:, which * rank : (which + 1) * rank]
                 if count == leaves:
                     update = update + couple_sum[2 * i + which]
                 below_here.append(update.astype(bf16))
         parents = below_here
+    local = jnp.concatenate([parent.astype(f32) for parent in parents], axis=0).astype(bf16)
+    local = dot_nt(local, shuffle)
     for leaf in range(leaves):
         lanes = pl.ds(leaf * leaf_size, leaf_size)
-        out[:, lanes] = out[:, lanes] + dot(parents[leaf], basis[leaf])
+        mine = local[8 * leaf : 8 * leaf + 8].astype(bf16)
+        out[:, lanes] = out[:, lanes] + dot(mine, basis[leaf])
 
     for copy in win_copies + coef_copies:
         copy.wait_send()
@@ -495,15 +531,17 @@
             pltpu.VMEM((2, 16, 128), bf16),
             pltpu.VMEM((4, 16, 128), bf16),
             pltpu.VMEM((leaves, rank, leaf_size), bf16),
-            pltpu.VMEM(((2 * leaves - 2) * rank, rank), bf16),
+            pltpu.VMEM((2 * leaves - 2, rank * rank), bf16),
             pltpu.VMEM((leaves, couples, rank * rank), bf16),
-            pltpu.VMEM((3 * leaves, leaf_size, 32), bf16),
-            pltpu.VMEM((leaves, 32, leaf_size), bf16),
+            pltpu.VMEM((2 * leaves - 2, rank, rank), bf16),
+            pltpu.VMEM((8, rank * rank), f32),
+            pltpu.VMEM(((2 * leaves - 2) * rank // 2, 128), f32),
+            pltpu.VMEM((8, rank, rank), bf16),
+            pltpu.VMEM((leaves, 48, leaf_size), bf16),
             pltpu.VMEM((8, 2048), f32),
             pltpu.VMEM((8 * leaves, 128), f32),
             pltpu.VMEM((8 * rank, 128), f32),
             pltpu.VMEM((8 * rank, leaves * couples), bf16),
-            pltpu.VMEM((leaves, 8, rank), f32),
             pltpu.VMEM((leaves, 8, rank), f32),
             dma((3,)),
             dma((2,)),
@@ -521,15 +559,15 @@
         name="h2_product",
     )
     return call(
-        near_list,
+        near_list.T,
         near_count,
-        couple_list.reshape(1, leaves * couples),
+        couple_list.T,
         points,
         vectors,
-        upper_transfer.reshape(2 * rank, rank),
-        upper_couple.reshape(6 * rank, rank),
+        upper_transfer,
+        upper_couple.transpose(1, 0, 2),
         leaf_basis,
-        local_transfer.reshape((2 * leaves - 2) * rank, rank),
+        local_transfer.reshape(2 * leaves - 2, rank * rank),
         couple_block,
     )
 

time: 132 us -> 120 us (0.909)
  local copies, waits for them, and re-layouts: 11.9 us -> 1.87 us
    reshape x4 -> x0, local copies, waits for them, and re-layouts: 7.06 us -> none  [the longest x1 4.2 us: shards(): local_transfer.reshape((2 * leaves - 2) * rank, rank)]
    unnamed x4 -> x1, local copies, waits for them, and re-layouts: 4.87 us -> 1.87 us
where the time goes in v2:
time: 120 us; the launch traced here: 119 us
  Pallas kernels  117 us (98%)
  local copies, waits for them, and re-layouts  1.87 us (2%)
    pallas_call x1, Pallas kernels, shards(): call(near_list.T, near_count, couple_list.T, points, vectors, upper_trans...  117 us

profile of v2, /device:TPU:1, one launch (start us, length us, event | category | flops | bytes accessed | tf_op | source)
XLA Modules:
  0.0 119.3 jit_solution(10419085047268898710)
XLA Ops:
  0.0 117.4 %h2_product.1 = f32[8,16384]{1,0:T(8,128)} custom-call(s32[16,64]{1,0:T(8,128)} %bitcast.6, s32[64]{0:T(128)} %count_ref.1, s32[16,64]{1,0:T(8,128)} %bitcast.7, f32[3,16384]{1,0:T(4,128)} %points.1, bf16[8,16384]{1,0:T(8,128)(2,1)} %vectors.1, bf16[2,4096]{1,0:T(2,128)(2,1)} %up_mats.1, bf16[3,2,4096]{2,1,0:T(2,128)(2,1)} %bitcast.5, ...), custom_call_target="tpu_custom_call" | custom-call | tf_op jit(solution)/shard_map/h2_product/pallas_call | solution.py:561
  117.4 1.9 %copy.12 = f32[8,16384]{1,0:T(8,128)} copy(f32[8,16384]{1,0:T(8,128)} %h2_product.1) | data formatting | bytes 1048576

commit v3 on v2

--- a/solution.py
+++ b/solution.py
@@ -96,6 +96,7 @@
     wide_scr,
     upper,
     tgt_feat,
+    own_kernels,
     rows_scr,
     coef_scr,
     coef_t,
@@ -125,7 +126,7 @@
         pltpu.make_async_copy(transfer_hbm, stored, load_sem.at[1]),
         pltpu.make_async_copy(couple_hbm, couple, load_sem.at[2]),
     ]
-    for load in loads:
+    for load in loads[:2]:
         load.start()
 
     kids[...] = jnp.zeros_like(kids)
@@ -211,6 +212,7 @@
         )
         copy.start()
         win_copies.append(copy)
+    loads[2].start()
 
     loads[0].wait()
     coef_scr[...] = jnp.zeros_like(coef_scr)
@@ -221,7 +223,8 @@
         block = coef_scr[pl.ds(v, leaves, stride=8), :]
         block = jnp.concatenate([block, jnp.zeros_like(block)], axis=0)
         coef_t[pl.ds(v, rank, stride=8), :] = block.T[0:rank]
-    coef_window[2] = coef_t[...].astype(bf16)
+    folded = coef_t[0 : 4 * rank] + pltpu.roll(coef_t[4 * rank : 8 * rank], rank, 1)
+    coef_window[2] = folded.astype(bf16)
     coef_copies = []
     for k, shift in enumerate((1, -1, 2, -2)):
         copy = pltpu.make_async_remote_copy(
@@ -377,6 +380,55 @@
                     outgoing.at[2 + which], downs.at[slot], down_recv.at[slot]
                 ).start()
 
+    scale = unit / math.sqrt(leaf_size * (slots + 1))
+
+    def kernel_of(v, target):
+        ones = jnp.ones((16, leaf_size), bf16)
+        d = dot_tn(jnp.concatenate([v, v, ones], axis=0), target)
+        return lax.rsqrt(d).astype(bf16)
+
+    def lanes_of(leaf):
+        return pl.ds(pl.multiple_of(leaf * leaf_size, leaf_size), leaf_size)
+
+    @pl.loop(0, leaves // 8)
+    def _(i):
+        for k in range(8):
+            leaf = i * 8 + k
+            own_kernels[leaf] = kernel_of(window[leaves + leaf], tgt_feat[leaf])
+
+    for copy in win_copies:
+        copy.wait_recv()
+    levels = devices.bit_length() - 1
+    together = 4
+    up_at = jnp.where(inner, levels - depth, -1)
+    down_at = jnp.where(inner, levels - 1 + depth, -1)
+
+    @pl.loop(0, leaves // together)
+    def _(i):
+        for k in range(together):
+            leaf = i * together + k
+            target = tgt_feat[leaf]
+            live = count_ref[leaf]
+            weights = [window[leaves + leaf]]
+            kernels = [own_kernels[leaf]]
+            for s in range(slots):
+                m = near_ref[s, leaf] - (me - 1) * leaves
+                m = jnp.minimum(jnp.maximum(m, 0), 3 * leaves - 1)
+                v = window[m]
+                kernels.append(kernel_of(v, target))
+                used = jnp.minimum(jnp.maximum(live - s, 0), 1).astype(f32)
+                weights.append((v.astype(f32) * used).astype(bf16))
+            near = dot(jnp.concatenate(weights, axis=1), jnp.concatenate(kernels, axis=0))
+            out[:, lanes_of(leaf)] = near[0:8] * scale
+
+        @pl.when(i == up_at)
+        def _():
+            upward()
+
+        @pl.when(i == down_at)
+        def _():
+            downward()
+
     for copy in coef_copies:
         copy.wait_recv()
     couples = couple.shape[1]
@@ -387,18 +439,24 @@
     row = lax.broadcasted_iota(jnp.int32, (leaves, columns), 0)
     lane = lax.broadcasted_iota(jnp.int32, (leaves, columns), 1)
     spread = dot(both, jnp.where(row == lax.div(lane, couples), 1.0, 0.0).astype(bf16))
-    spread = spread[0:couples] * 128.0 + spread[couples:]
+    spread = spread[0:couples] * float(leaves) + spread[couples:]
     row = lax.broadcasted_iota(jnp.int32, (couples, columns), 0)
     lane = lax.broadcasted_iota(jnp.int32, (couples, columns), 1)
     spread = jnp.where(row == lax.rem(lane, couples), spread, 0.0)
     spread = jnp.sum(spread, axis=0, keepdims=True).astype(jnp.int32)
-    total = None
-    for k in range(2 * REACH + 1):
-        row = lax.broadcasted_iota(jnp.int32, (128, spread.shape[1]), 0) + 128 * k
-        chosen = jnp.where(row == spread, 1.0, 0.0).astype(bf16)
-        part = dot(coef_window[k], chosen)
-        total = part if total is None else total + part
-    gathered[...] = total.astype(bf16)
+    blocks = [coef_window[k] for k in range(2 * REACH + 1)]
+    blocks = jnp.concatenate(blocks, axis=1)
+    row = lax.broadcasted_iota(jnp.int32, (leaves, columns), 0)
+    nothing = jnp.zeros((leaves, columns), bf16)
+    chosen = [
+        jnp.where(row + leaves * k == spread, 1.0, 0.0).astype(bf16) for k in range(2 * REACH + 1)
+    ]
+    for part in range(2):
+        masks = []
+        for pick in chosen:
+            masks += [nothing, pick] if part else [pick, nothing]
+        found = dot(blocks, jnp.concatenate(masks, axis=0))
+        gathered[pl.ds(part * 4 * rank, 4 * rank)] = found.astype(bf16)
 
     group = 128 // couples
     loads[2].wait()
@@ -425,45 +483,6 @@
     coarse = flat.astype(bf16)
     flat = dot(coarse, shuffle) + dot((flat - coarse.astype(f32)).astype(bf16), shuffle)
     couple_sum[...] = flat.reshape(leaves, 8, rank)
-
-    for copy in win_copies:
-        copy.wait_recv()
-
-    scale = unit / math.sqrt(leaf_size * (slots + 1))
-    levels = devices.bit_length() - 1
-    gap = 3
-    up_at = jnp.where(inner, 2 + gap * (levels - 1 - depth), -1)
-    down_at = jnp.where(inner, 2 + gap * (levels + depth), -1)
-
-    @pl.loop(0, leaves)
-    def _(leaf):
-        target = tgt_feat[leaf]
-        live = count_ref[leaf]
-        ones = jnp.ones((16, leaf_size), bf16)
-        weights = []
-        kernels = []
-        for s in range(slots + 1):
-            m = leaf + leaves
-            if s:
-                m = near_ref[s - 1, leaf] - (me - 1) * leaves
-                m = jnp.minimum(jnp.maximum(m, 0), 3 * leaves - 1)
-            v = window[m]
-            d = dot_tn(jnp.concatenate([v, v, ones], axis=0), target)
-            kernels.append(lax.rsqrt(d).astype(bf16))
-            if s:
-                used = jnp.minimum(jnp.maximum(live - (s - 1), 0), 1).astype(f32)
-                v = (v.astype(f32) * used).astype(bf16)
-            weights.append(v)
-        near = dot(jnp.concatenate(weights, axis=1), jnp.concatenate(kernels, axis=0))
-        out[:, pl.ds(pl.multiple_of(leaf * leaf_size, leaf_size), leaf_size)] = near[0:8] * scale
-
-        @pl.when(leaf == up_at)
-        def _():
-            upward()
-
-        @pl.when(leaf == down_at)
-        def _():
-            downward()
 
     wait_down(1)
     parents = [downs[1][0:8, 0:rank]]
@@ -526,7 +545,7 @@
         out_specs=vmem,
         scratch_shapes=[
             pltpu.VMEM((3 * leaves, 16, leaf_size), bf16),
-            pltpu.VMEM((2 * REACH + 1, 8 * rank, 128), bf16),
+            pltpu.VMEM((2 * REACH + 1, 4 * rank, 128), bf16),
             pltpu.VMEM((6, 16, 128), bf16),
             pltpu.VMEM((2, 16, 128), bf16),
             pltpu.VMEM((4, 16, 128), bf16),
@@ -538,6 +557,7 @@
             pltpu.VMEM(((2 * leaves - 2) * rank // 2, 128), f32),
             pltpu.VMEM((8, rank, rank), bf16),
             pltpu.VMEM((leaves, 48, leaf_size), bf16),
+            pltpu.VMEM((leaves, leaf_size, leaf_size), bf16),
             pltpu.VMEM((8, 2048), f32),
             pltpu.VMEM((8 * leaves, 128), f32),
             pltpu.VMEM((8 * rank, 128), f32),

time: 120 us -> 98.6 us (0.82)
  Pallas kernels: 117 us -> 96.5 us
    pallas_call x1, Pallas kernels: 117 us -> 96.5 us  [shards(): call(near_list.T, near_count, couple_list.T, points, vectors, upper_trans...]
where the time goes in v3:
time: 98.6 us; the launch traced here: 98.4 us
  Pallas kernels  96.5 us (98%)
  local copies, waits for them, and re-layouts  1.87 us (2%)
    pallas_call x1, Pallas kernels, shards(): call(near_list.T, near_count, couple_list.T, points, vectors, upper_trans...  96.5 us

profile of v3, /device:TPU:1, one launch (start us, length us, event | category | flops | bytes accessed | tf_op | source)
XLA Modules:
  0.0 98.4 jit_solution(1036702480406269245)
XLA Ops:
  0.0 96.5 %h2_product.1 = f32[8,16384]{1,0:T(8,128)} custom-call(s32[16,64]{1,0:T(8,128)} %bitcast.6, s32[64]{0:T(128)} %count_ref.1, s32[16,64]{1,0:T(8,128)} %bitcast.7, f32[3,16384]{1,0:T(4,128)} %points.1, bf16[8,16384]{1,0:T(8,128)(2,1)} %vectors.1, bf16[2,4096]{1,0:T(2,128)(2,1)} %up_mats.1, bf16[3,2,4096]{2,1,0:T(2,128)(2,1)} %bitcast.5, ...), custom_call_target="tpu_custom_call" | custom-call | tf_op jit(solution)/shard_map/h2_product/pallas_call | solution.py:581
  96.5 1.9 %copy.12 = f32[8,16384]{1,0:T(8,128)} copy(f32[8,16384]{1,0:T(8,128)} %h2_product.1) | data formatting | bytes 1048576

commit v4 on v3

--- a/solution.py
+++ b/solution.py
@@ -41,10 +41,18 @@
     high = round16(own)
     kept = jnp.where(edge, 0.0, high + round16(own - high))
     norm = 0.5 * jnp.sum(kept * kept, axis=0, keepdims=True) + 0.5 * soft_sq * unit * unit
-    norm = jnp.broadcast_to(norm, own.shape)
+    return edge, kept, jnp.broadcast_to(norm, own.shape)
+
+
+def source_rows(own, row):
+    edge, kept, norm = leaf_rows(own, row)
     source = jnp.where(edge, norm, kept)
     high = round16(source)
-    source = jnp.where(row < 4, high, source - high)
+    return jnp.where(row < 4, high, source - high)
+
+
+def target_rows(own, row):
+    edge, kept, norm = leaf_rows(own, row)
     facing = jnp.where(edge, 1.0, kept * -2.0)
     facing_high = round16(facing)
     n_one = round16(norm)
@@ -53,7 +61,7 @@
     norms = jnp.where(row == 0, n_one, jnp.where(row < 3, norms, 0.0))
     nothing = jnp.zeros_like(own)
     target = [nothing, facing_high, nothing, facing - facing_high, norms, nothing]
-    return source, jnp.concatenate(target, axis=0)
+    return jnp.concatenate(target, axis=0)
 
 
 def shuffled(rows, columns, shift):
@@ -182,21 +190,25 @@
 
     step = 8
 
-    @pl.loop(0, leaves // step)
-    def _(i):
-        lanes = pl.ds(pl.multiple_of(i * step * leaf_size, step * leaf_size), step * leaf_size)
+    def own_rows(lanes):
         own = (points[:, lanes] - 0.5) * unit
-        rows_scr[...] = jnp.zeros_like(rows_scr)
         rows_scr[0:3] = own
         rows_scr[4:7] = own
         both = rows_scr[...]
-        source, target = leaf_rows(both, lax.broadcasted_iota(jnp.int32, both.shape, 0))
+        return both, lax.broadcasted_iota(jnp.int32, both.shape, 0)
+
+    def lanes_from(i):
+        return pl.ds(pl.multiple_of(i * step * leaf_size, step * leaf_size), step * leaf_size)
+
+    rows_scr[...] = jnp.zeros_like(rows_scr)
+
+    @pl.loop(0, leaves // step)
+    def _(i):
+        lanes = lanes_from(i)
+        source = source_rows(*own_rows(lanes))
         packed = jnp.concatenate([vectors[:, lanes].astype(f32), source], axis=0).astype(bf16)
-        target = target.astype(bf16)
         for k in range(step):
-            part = slice(k * leaf_size, (k + 1) * leaf_size)
-            window[leaves + i * step + k] = packed[:, part]
-            tgt_feat[i * step + k] = target[:, part]
+            window[leaves + i * step + k] = packed[:, k * leaf_size : (k + 1) * leaf_size]
 
     pl.semaphore_wait(barrier, expected)
 
@@ -213,6 +225,12 @@
         copy.start()
         win_copies.append(copy)
     loads[2].start()
+
+    @pl.loop(0, leaves // step)
+    def _(i):
+        target = target_rows(*own_rows(lanes_from(i))).astype(bf16)
+        for k in range(step):
+            tgt_feat[i * step + k] = target[:, k * leaf_size : (k + 1) * leaf_size]
 
     loads[0].wait()
     coef_scr[...] = jnp.zeros_like(coef_scr)
@@ -396,14 +414,73 @@
             leaf = i * 8 + k
             own_kernels[leaf] = kernel_of(window[leaves + leaf], tgt_feat[leaf])
 
+    couples = couple.shape[1]
+    columns = leaves * couples
+    group = 128 // couples
+    pieces = 2 * (leaves // group)
+    chunks = rank * rank // 128 // 2
+    gathered[...] = jnp.zeros_like(gathered)
+
+    def gather():
+        for copy in coef_copies:
+            copy.wait_recv()
+        places = couple_ids[...] - (me - REACH) * leaves
+        owner = lax.div(places, leaves)
+        both = jnp.concatenate([owner, places - owner * leaves], axis=0).astype(bf16)
+        row = lax.broadcasted_iota(jnp.int32, (leaves, columns), 0)
+        lane = lax.broadcasted_iota(jnp.int32, (leaves, columns), 1)
+        spread = dot(both, jnp.where(row == lax.div(lane, couples), 1.0, 0.0).astype(bf16))
+        spread = spread[0:couples] * float(leaves) + spread[couples:]
+        row = lax.broadcasted_iota(jnp.int32, (couples, columns), 0)
+        lane = lax.broadcasted_iota(jnp.int32, (couples, columns), 1)
+        spread = jnp.where(row == lax.rem(lane, couples), spread, 0.0)
+        spread = jnp.sum(spread, axis=0, keepdims=True).astype(jnp.int32)
+        blocks = [coef_window[k] for k in range(2 * REACH + 1)]
+        blocks = jnp.concatenate(blocks, axis=1)
+        row = lax.broadcasted_iota(jnp.int32, (leaves, columns), 0)
+        nothing = jnp.zeros((leaves, columns), bf16)
+        chosen = [
+            jnp.where(row + leaves * k == spread, 1.0, 0.0).astype(bf16) for k in range(2 * REACH + 1)
+        ]
+        for part in range(2):
+            masks = []
+            for pick in chosen:
+                masks += [nothing, pick] if part else [pick, nothing]
+            found = dot(blocks, jnp.concatenate(masks, axis=0))
+            gathered[pl.ds(part * 4 * rank, 4 * rank)] = found.astype(bf16)
+
+    def couple_piece(piece):
+        g = lax.div(piece, 2)
+        h = lax.rem(piece, 2)
+        row = lax.broadcasted_iota(jnp.int32, (128, 128), 0)
+        lane = lax.broadcasted_iota(jnp.int32, (128, 128), 1)
+        mask = jnp.where(lax.div(row, 16) == lax.div(lane, 16), 1.0, 0.0).astype(bf16)
+        lefts = []
+        rights = []
+        lanes = pl.ds(pl.multiple_of(g * 128, 128), 128)
+        for k in range(chunks):
+            j = h * chunks + k
+            x = gathered[pl.ds(pl.multiple_of(16 * j, 16), 16), lanes]
+            lefts.append(jnp.concatenate([x] * group, axis=0) * mask)
+            block = couple[pl.ds(g * group, group), :, pl.ds(pl.multiple_of(128 * j, 128), 128)]
+            rights.append(block.reshape(128, 128))
+        r = dot(jnp.concatenate(lefts, axis=1), jnp.concatenate(rights, axis=0))
+        r = r.reshape(group, 16, 128)
+        r = r[:, 0:8, 0:rank] + r[:, 8:16, rank : 2 * rank]
+        here = pl.ds(g * group, group)
+        couple_sum[here] = couple_sum[here] * h.astype(f32) + r
+
     for copy in win_copies:
         copy.wait_recv()
     levels = devices.bit_length() - 1
     together = 4
+    steps = leaves // together
+    loads[2].wait()
+    couple_sum[...] = jnp.zeros_like(couple_sum)
     up_at = jnp.where(inner, levels - depth, -1)
     down_at = jnp.where(inner, levels - 1 + depth, -1)
 
-    @pl.loop(0, leaves // together)
+    @pl.loop(0, steps)
     def _(i):
         for k in range(together):
             leaf = i * together + k
@@ -420,6 +497,11 @@
                 weights.append((v.astype(f32) * used).astype(bf16))
             near = dot(jnp.concatenate(weights, axis=1), jnp.concatenate(kernels, axis=0))
             out[:, lanes_of(leaf)] = near[0:8] * scale
+        couple_piece(jnp.maximum(i - 1, 0))
+
+        @pl.when(i == 0)
+        def _():
+            gather()
 
         @pl.when(i == up_at)
         def _():
@@ -429,56 +511,7 @@
         def _():
             downward()
 
-    for copy in coef_copies:
-        copy.wait_recv()
-    couples = couple.shape[1]
-    columns = leaves * couples
-    places = couple_ids[...] - (me - REACH) * leaves
-    owner = lax.div(places, leaves)
-    both = jnp.concatenate([owner, places - owner * leaves], axis=0).astype(bf16)
-    row = lax.broadcasted_iota(jnp.int32, (leaves, columns), 0)
-    lane = lax.broadcasted_iota(jnp.int32, (leaves, columns), 1)
-    spread = dot(both, jnp.where(row == lax.div(lane, couples), 1.0, 0.0).astype(bf16))
-    spread = spread[0:couples] * float(leaves) + spread[couples:]
-    row = lax.broadcasted_iota(jnp.int32, (couples, columns), 0)
-    lane = lax.broadcasted_iota(jnp.int32, (couples, columns), 1)
-    spread = jnp.where(row == lax.rem(lane, couples), spread, 0.0)
-    spread = jnp.sum(spread, axis=0, keepdims=True).astype(jnp.int32)
-    blocks = [coef_window[k] for k in range(2 * REACH + 1)]
-    blocks = jnp.concatenate(blocks, axis=1)
-    row = lax.broadcasted_iota(jnp.int32, (leaves, columns), 0)
-    nothing = jnp.zeros((leaves, columns), bf16)
-    chosen = [
-        jnp.where(row + leaves * k == spread, 1.0, 0.0).astype(bf16) for k in range(2 * REACH + 1)
-    ]
-    for part in range(2):
-        masks = []
-        for pick in chosen:
-            masks += [nothing, pick] if part else [pick, nothing]
-        found = dot(blocks, jnp.concatenate(masks, axis=0))
-        gathered[pl.ds(part * 4 * rank, 4 * rank)] = found.astype(bf16)
-
-    group = 128 // couples
-    loads[2].wait()
-    chunks = rank * rank // 128
-
-    @pl.loop(0, leaves // group)
-    def _(g):
-        row = lax.broadcasted_iota(jnp.int32, (128, 128), 0)
-        lane = lax.broadcasted_iota(jnp.int32, (128, 128), 1)
-        mask = jnp.where(lax.div(row, 16) == lax.div(lane, 16), 1.0, 0.0).astype(bf16)
-        lefts = []
-        rights = []
-        lanes = pl.ds(pl.multiple_of(g * 128, 128), 128)
-        for j in range(chunks):
-            x = gathered[pl.ds(16 * j, 16), lanes]
-            lefts.append(jnp.concatenate([x] * group, axis=0) * mask)
-            block = couple[pl.ds(g * group, group), :, pl.ds(128 * j, 128)]
-            rights.append(block.reshape(128, 128))
-        r = dot(jnp.concatenate(lefts, axis=1), jnp.concatenate(rights, axis=0))
-        r = r.reshape(group, 16, 128)
-        couple_sum[pl.ds(g * group, group)] = r[:, 0:8, 0:rank] + r[:, 8:16, rank : 2 * rank]
-
+    couple_piece(pieces - 1)
     flat = couple_sum[...].reshape(8 * leaves, rank)
     coarse = flat.astype(bf16)
     flat = dot(coarse, shuffle) + dot((flat - coarse.astype(f32)).astype(bf16), shuffle)

time: 98.6 us -> 96.4 us (0.978)
  Pallas kernels: 96.5 us -> 94.4 us
    pallas_call x1, Pallas kernels: 96.5 us -> 94.4 us  [shards(): call(near_list.T, near_count, couple_list.T, points, vectors, upper_trans...]
where the time goes in v4:
time: 96.4 us; the launch traced here: 96.2 us
  Pallas kernels  94.4 us (98%)
  local copies, waits for them, and re-layouts  1.87 us (2%)
    pallas_call x1, Pallas kernels, shards(): call(near_list.T, near_count, couple_list.T, points, vectors, upper_trans...  94.4 us

profile of v4, /device:TPU:1, one launch (start us, length us, event | category | flops | bytes accessed | tf_op | source)
XLA Modules:
  0.0 96.2 jit_solution(11942465215697591780)
XLA Ops:
  0.0 94.4 %h2_product.1 = f32[8,16384]{1,0:T(8,128)} custom-call(s32[16,64]{1,0:T(8,128)} %bitcast.6, s32[64]{0:T(128)} %count_ref.1, s32[16,64]{1,0:T(8,128)} %bitcast.7, f32[3,16384]{1,0:T(4,128)} %points.1, bf16[8,16384]{1,0:T(8,128)(2,1)} %vectors.1, bf16[2,4096]{1,0:T(2,128)(2,1)} %up_mats.1, bf16[3,2,4096]{2,1,0:T(2,128)(2,1)} %bitcast.5, ...), custom_call_target="tpu_custom_call" | custom-call | tf_op jit(solution)/shard_map/h2_product/pallas_call | solution.py:614
  94.4 1.9 %copy.12 = f32[8,16384]{1,0:T(8,128)} copy(f32[8,16384]{1,0:T(8,128)} %h2_product.1) | data formatting | bytes 1048576

commit v5 on v4

--- a/solution.py
+++ b/solution.py
@@ -414,6 +414,12 @@
             leaf = i * 8 + k
             own_kernels[leaf] = kernel_of(window[leaves + leaf], tgt_feat[leaf])
 
+    order = devices.bit_length() - 2 - depth
+
+    @pl.when(inner & (order == 0))
+    def _():
+        upward()
+
     couples = couple.shape[1]
     columns = leaves * couples
     group = 128 // couples
@@ -472,52 +478,70 @@
 
     for copy in win_copies:
         copy.wait_recv()
-    levels = devices.bit_length() - 1
-    together = 4
-    steps = leaves // together
     loads[2].wait()
     couple_sum[...] = jnp.zeros_like(couple_sum)
-    up_at = jnp.where(inner, levels - depth, -1)
-    down_at = jnp.where(inner, levels - 1 + depth, -1)
-
-    @pl.loop(0, steps)
+
+    @pl.when(inner & (order == 1))
+    def _():
+        upward()
+
+    def near_of(leaf):
+        target = tgt_feat[leaf]
+        live = count_ref[leaf]
+        weights = [window[leaves + leaf]]
+        kernels = [own_kernels[leaf]]
+        for s in range(slots):
+            m = near_ref[s, leaf] - (me - 1) * leaves
+            m = jnp.minimum(jnp.maximum(m, 0), 3 * leaves - 1)
+            v = window[m]
+            kernels.append(kernel_of(v, target))
+            used = jnp.minimum(jnp.maximum(live - s, 0), 1).astype(f32)
+            weights.append((v.astype(f32) * used).astype(bf16))
+        near = dot(jnp.concatenate(weights, axis=1), jnp.concatenate(kernels, axis=0))
+        out[:, lanes_of(leaf)] = near[0:8] * scale
+
+    wide, narrow, turns = 8, 4, 5
+
+    @pl.loop(0, turns)
     def _(i):
-        for k in range(together):
-            leaf = i * together + k
-            target = tgt_feat[leaf]
-            live = count_ref[leaf]
-            weights = [window[leaves + leaf]]
-            kernels = [own_kernels[leaf]]
-            for s in range(slots):
-                m = near_ref[s, leaf] - (me - 1) * leaves
-                m = jnp.minimum(jnp.maximum(m, 0), 3 * leaves - 1)
-                v = window[m]
-                kernels.append(kernel_of(v, target))
-                used = jnp.minimum(jnp.maximum(live - s, 0), 1).astype(f32)
-                weights.append((v.astype(f32) * used).astype(bf16))
-            near = dot(jnp.concatenate(weights, axis=1), jnp.concatenate(kernels, axis=0))
-            out[:, lanes_of(leaf)] = near[0:8] * scale
-        couple_piece(jnp.maximum(i - 1, 0))
+        for k in range(wide):
+            near_of(i * wide + k)
+        first = 2 * jnp.maximum(i - 1, 0)
+        couple_piece(first)
+        couple_piece(first + 1)
 
         @pl.when(i == 0)
         def _():
             gather()
 
-        @pl.when(i == up_at)
+        @pl.when(inner & (order == i + 2))
         def _():
             upward()
 
-        @pl.when(i == down_at)
+        @pl.when(inner & (depth == i - 2))
         def _():
             downward()
 
-    couple_piece(pieces - 1)
+    @pl.loop(0, turns)
+    def _(i):
+        for k in range(narrow):
+            near_of(turns * wide + i * narrow + k)
+        couple_piece(2 * (turns - 1) + i)
+
+        @pl.when(inner & (depth == i + turns - 2))
+        def _():
+            downward()
+
+    wait_down(1)
+    for leaf in range(turns * (wide + narrow), leaves):
+        near_of(leaf)
+    for piece in range(2 * (turns - 1) + turns, pieces):
+        couple_piece(jnp.int32(piece))
     flat = couple_sum[...].reshape(8 * leaves, rank)
     coarse = flat.astype(bf16)
     flat = dot(coarse, shuffle) + dot((flat - coarse.astype(f32)).astype(bf16), shuffle)
     couple_sum[...] = flat.reshape(leaves, 8, rank)
 
-    wait_down(1)
     parents = [downs[1][0:8, 0:rank]]
     while len(parents) < leaves:
         below_here = []

time: 96.4 us -> 101 us (1.048); the launches traced: 96.2 us -> 99.6 us
  Pallas kernels: 94.4 us -> 97.7 us
    pallas_call x1, Pallas kernels: 94.4 us -> 97.7 us  [shards(): call(near_list.T, near_count, couple_list.T, points, vectors, upper_trans...]
where the time goes in v5:
time: 101 us; the launch traced here: 99.6 us
  Pallas kernels  97.7 us (97%)
  local copies, waits for them, and re-layouts  1.87 us (2%)
    pallas_call x1, Pallas kernels, shards(): call(near_list.T, near_count, couple_list.T, points, vectors, upper_trans...  97.7 us

profile of v5, /device:TPU:1, one launch (start us, length us, event | category | flops | bytes accessed | tf_op | source)
XLA Modules:
  0.0 99.6 jit_solution(1180267577123966244)
XLA Ops:
  0.0 97.7 %h2_product.1 = f32[8,16384]{1,0:T(8,128)} custom-call(s32[16,64]{1,0:T(8,128)} %bitcast.6, s32[64]{0:T(128)} %count_ref.1, s32[16,64]{1,0:T(8,128)} %bitcast.7, f32[3,16384]{1,0:T(4,128)} %points.1, bf16[8,16384]{1,0:T(8,128)(2,1)} %vectors.1, bf16[2,4096]{1,0:T(2,128)(2,1)} %up_mats.1, bf16[3,2,4096]{2,1,0:T(2,128)(2,1)} %bitcast.5, ...), custom_call_target="tpu_custom_call" | custom-call | tf_op jit(solution)/shard_map/h2_product/pallas_call | solution.py:638
  97.7 1.9 %copy.12 = f32[8,16384]{1,0:T(8,128)} copy(f32[8,16384]{1,0:T(8,128)} %h2_product.1) | data formatting | bytes 1048576

commit v6 on v4

--- a/solution.py
+++ b/solution.py
@@ -480,8 +480,7 @@
     up_at = jnp.where(inner, levels - depth, -1)
     down_at = jnp.where(inner, levels - 1 + depth, -1)
 
-    @pl.loop(0, steps)
-    def _(i):
+    def turn(i):
         for k in range(together):
             leaf = i * together + k
             target = tgt_feat[leaf]
@@ -499,6 +498,10 @@
             out[:, lanes_of(leaf)] = near[0:8] * scale
         couple_piece(jnp.maximum(i - 1, 0))
 
+    @pl.loop(0, steps - 1)
+    def _(i):
+        turn(i)
+
         @pl.when(i == 0)
         def _():
             gather()
@@ -511,13 +514,14 @@
         def _():
             downward()
 
-    couple_piece(pieces - 1)
+    wait_down(1)
+    turn(jnp.int32(steps - 1))
+    couple_piece(jnp.int32(pieces - 1))
     flat = couple_sum[...].reshape(8 * leaves, rank)
     coarse = flat.astype(bf16)
     flat = dot(coarse, shuffle) + dot((flat - coarse.astype(f32)).astype(bf16), shuffle)
     couple_sum[...] = flat.reshape(leaves, 8, rank)
 
-    wait_down(1)
     parents = [downs[1][0:8, 0:rank]]
     while len(parents) < leaves:
         below_here = []

time: 96.4 us -> 95.8 us (level)
  no operation moved by 1% of the time
where the time goes in v6:
time: 95.8 us; the launch traced here: 95.6 us
  Pallas kernels  93.7 us (98%)
  local copies, waits for them, and re-layouts  1.87 us (2%)
    pallas_call x1, Pallas kernels, shards(): call(near_list.T, near_count, couple_list.T, points, vectors, upper_trans...  93.7 us

profile of v6, /device:TPU:1, one launch (start us, length us, event | category | flops | bytes accessed | tf_op | source)
XLA Modules:
  0.0 95.6 jit_solution(12387535981675577)
XLA Ops:
  0.0 93.7 %h2_product.1 = f32[8,16384]{1,0:T(8,128)} custom-call(s32[16,64]{1,0:T(8,128)} %bitcast.6, s32[64]{0:T(128)} %count_ref.1, s32[16,64]{1,0:T(8,128)} %bitcast.7, f32[3,16384]{1,0:T(4,128)} %points.1, bf16[8,16384]{1,0:T(8,128)(2,1)} %vectors.1, bf16[2,4096]{1,0:T(2,128)(2,1)} %up_mats.1, bf16[3,2,4096]{2,1,0:T(2,128)(2,1)} %bitcast.5, ...), custom_call_target="tpu_custom_call" | custom-call | tf_op jit(solution)/shard_map/h2_product/pallas_call | solution.py:618
  93.7 1.9 %copy.12 = f32[8,16384]{1,0:T(8,128)} copy(f32[8,16384]{1,0:T(8,128)} %h2_product.1) | data formatting | bytes 1048576
